TPU v7x, 512 devices: a whole 4x4x16 slice. The times are simulated.
512 devices in a mesh: lon: 32 (over z_hi, y, core), lat: 16 (over x, z_lo).
Axes of the slice: x: 4, y: 4, z: 16 (z_hi: 4, z_lo: 4; z = z_hi * 4 + z_lo), core: 2. Of those that a mesh axis runs over, the one named last changes fastest.
Arguments:
- zonal_flow_middle: float32 [8, 512, 8192], P(None, 'lat', 'lon'), may hold values from -6 to 6
- meridional_flow_middle: float32 [8, 512, 8192], P(None, 'lat', 'lon'), may hold values from -6 to 6
- heat_content: float32 [8, 512, 8192], P(None, 'lat', 'lon'), may hold values from -6 to 6
- ocean_strata_number: int32 [512, 8192], P('lat', 'lon'), may hold values from 0 to 8
- former_free_elevation: float32 [512, 8192], P('lat', 'lon'), may hold values from -6 to 6
Outputs:
- zonal_new: float32 [8, 512, 8192], P(None, 'lat', 'lon')
- meridional_new: float32 [8, 512, 8192], P(None, 'lat', 'lon')
- temperature_new: float32 [8, 512, 8192], P(None, 'lat', 'lon')
- surface_pressure: float32 [512, 8192], P('lat', 'lon')
All inputs are finite; a program needn't handle non-finite values.
Results may differ from a plain program's by a relative error of at most 0.035.
Values sent between devices are 32-bit elements; how exact they have to be, the bound alone decides.
A program may use at most 64 MiB of HBM per device.

v0:
```python
import jax
import jax.numpy as jnp
from jax import lax
from jax.sharding import PartitionSpec as P

VERTICAL_STRATA = 8
GRIDS = 3
CYCLES = 3
SWEEPS = 4


TIME_STEP = 0.2
VISCOSITY = 1.0
DIFFUSIVITY = 1.0
CORIOLIS = 1.0
MASS_TERM = 0.05
GRAVITY_STEP = 0.5


def with_halo(block, sides, width):
    for axis, dim in sides:
        count = lax.axis_size(axis)
        forward = [(i, i + 1) for i in range(count - 1)]
        forward.append((count - 1, 0))
        backward = [(target, source) for source, target in forward]
        low = lax.ppermute(
            lax.slice_in_dim(block, block.shape[dim] - width, None, axis=dim), axis, forward
        )
        high = lax.ppermute(lax.slice_in_dim(block, 0, width, axis=dim), axis, backward)
        block = jnp.concatenate([low, block, high], axis=dim)
    return block


def clear_edges(padded, width):
    extent = lax.axis_size("lat")
    position = lax.axis_index("lat")
    height = padded.shape[-2]
    rows = jnp.arange(height)
    lower = jnp.logical_and(position == 0, rows < width)
    upper = jnp.logical_and(position == extent - 1, rows >= height - width)
    keep = jnp.where(jnp.logical_or(lower, upper), 0.0, 1.0).astype(jnp.float32)
    return padded * keep[:, None]


def padded_neighbours(padded):
    return (
        padded[..., 1:-1, 2:],
        padded[..., 1:-1, :-2],
        padded[..., 2:, 1:-1],
        padded[..., :-2, 1:-1],
    )


def field_rim(values):
    padded = with_halo(values, (("lon", 2), ("lat", 1)), 1)
    return padded_neighbours(clear_edges(padded, 1))


def plane_near(values):
    padded = with_halo(values, (("lon", 1), ("lat", 0)), 1)
    return padded_neighbours(clear_edges(padded, 1))


def rotation_rate(row_index, total_rows):
    return CORIOLIS * jnp.sin(jnp.pi * ((row_index + 0.5) / total_rows - 0.5))


def baroclinic(
    layer_index,
    eastward,
    northward,
    tracer,
    column_depth_count,
    near_east,
    near_north,
    near_tracer,
    near_depth,
    rotation,
):
    wet_cell = (layer_index < column_depth_count).astype(jnp.float32)
    face_open = [
        wet_cell * (layer_index < beside_depth).astype(jnp.float32) for beside_depth in near_depth
    ]

    def laplace(values, nearby):
        return (
            face_open[0] * (nearby[0] - values)
            + face_open[1] * (nearby[1] - values)
            + (face_open[2] * (nearby[2] - values) + face_open[3] * (nearby[3] - values))
        )

    east_flow = face_open[0] * (eastward + near_east[0]) * 0.5
    west_flow = face_open[1] * (near_east[1] + eastward) * 0.5
    north_flow = face_open[2] * (northward + near_north[2]) * 0.5
    south_flow = face_open[3] * (near_north[3] + northward) * 0.5
    transport = (
        east_flow * (tracer + near_tracer[0])
        - west_flow * (near_tracer[1] + tracer)
        + (north_flow * (tracer + near_tracer[2]) - south_flow * (near_tracer[3] + tracer))
    )
    advected_scalar = wet_cell * (
        tracer + TIME_STEP * (DIFFUSIVITY * laplace(tracer, near_tracer) - 0.5 * transport)
    )
    zonal_flow_guess = wet_cell * (
        eastward + TIME_STEP * (VISCOSITY * laplace(eastward, near_east) + rotation * northward)
    )
    meridional_flow_guess = wet_cell * (
        northward + TIME_STEP * (VISCOSITY * laplace(northward, near_north) - rotation * eastward)
    )
    return (zonal_flow_guess, meridional_flow_guess, advected_scalar)


def barotropic_source(near_east, near_north, column_depth_count, former_free_elevation):
    spread = 0.5 * (near_east[0] - near_east[1] + (near_north[2] - near_north[3]))
    wet_column = (column_depth_count > 0.5).astype(jnp.float32)
    return wet_column * (former_free_elevation - spread)


def fine_coefficients(column_depth_count, near_depth):
    column = column_depth_count * (1.0 / VERTICAL_STRATA)
    weights = [
        jnp.minimum(column, beside_depth * (1.0 / VERTICAL_STRATA)) for beside_depth in near_depth
    ]
    return (jnp.full_like(column, MASS_TERM), weights[0], weights[1], weights[2], weights[3])


def restrict(values):
    paired = values[..., 0::2, :] + values[..., 1::2, :]
    return paired[..., 0::2] + paired[..., 1::2]


def prolong(values):
    return jnp.repeat(jnp.repeat(values, 2, axis=-2), 2, axis=-1)


def coarse_coefficients(coeffs):
    mass_field, east_weight, west_weight, north_weight, south_weight = coeffs
    return (
        restrict(mass_field),
        east_weight[0::2, 1::2] + east_weight[1::2, 1::2],
        west_weight[0::2, 0::2] + west_weight[1::2, 0::2],
        north_weight[1::2, 0::2] + north_weight[1::2, 1::2],
        south_weight[0::2, 0::2] + south_weight[0::2, 1::2],
    )


def hierarchy(coeffs):
    grids_list = [coeffs]
    for grid_number in range(GRIDS):
        grids_list.append(coarse_coefficients(grids_list[-1]))
    return grids_list


def apply_operator(coeffs, pressure, nearby):
    mass_field, east_weight, west_weight, north_weight, south_weight = coeffs
    diagonal = mass_field + (east_weight + west_weight + (north_weight + south_weight))
    return diagonal * pressure - (
        east_weight * nearby[0]
        + west_weight * nearby[1]
        + (north_weight * nearby[2] + south_weight * nearby[3])
    )


def smooth_sweep(coeffs, pressure, source, nearby):
    mass_field, east_weight, west_weight, north_weight, south_weight = coeffs
    divisor = mass_field + 2.0 * (east_weight + west_weight + (north_weight + south_weight))
    if pressure is None:
        return source / divisor
    return pressure + (source - apply_operator(coeffs, pressure, nearby)) / divisor


def coarse_sweeps(coeffs, source, near_fn):
    pressure = smooth_sweep(coeffs, None, source, None)
    for sweep_number in range(SWEEPS - 1):
        pressure = smooth_sweep(coeffs, pressure, source, near_fn(pressure))
    return pressure


def multigrid_cycle(grids_list, grid_number, source, pressure, near_fn, coarse_solve):
    coeffs = grids_list[grid_number]
    if grid_number == len(grids_list) - 1:
        return coarse_solve(coeffs, source)
    pressure = smooth_sweep(
        coeffs, pressure, source, None if pressure is None else near_fn(pressure)
    )
    residual = source - apply_operator(coeffs, pressure, near_fn(pressure))
    correction = multigrid_cycle(
        grids_list, grid_number + 1, restrict(residual), None, near_fn, coarse_solve
    )
    pressure = pressure + prolong(correction)
    return smooth_sweep(coeffs, pressure, source, near_fn(pressure))


def corrected(wet_cell, zonal_flow_guess, meridional_flow_guess, near_surface):
    slope_east = 0.5 * (near_surface[0] - near_surface[1])
    slope_north = 0.5 * (near_surface[2] - near_surface[3])
    return (
        wet_cell * (zonal_flow_guess - GRAVITY_STEP * slope_east),
        wet_cell * (meridional_flow_guess - GRAVITY_STEP * slope_north),
    )


def shards(
    zonal_flow_middle,
    meridional_flow_middle,
    heat_content,
    ocean_strata_number,
    former_free_elevation,
):
    lat_cells = ocean_strata_number.shape[0]
    total_rows = lat_cells * lax.axis_size("lat")
    column_depth_count = ocean_strata_number.astype(jnp.float32)
    stacked = jnp.concatenate(
        [zonal_flow_middle, meridional_flow_middle, heat_content, column_depth_count[None]], axis=0
    )
    layers = jnp.arange(VERTICAL_STRATA).astype(jnp.float32)[:, None, None]
    nearby = field_rim(stacked)
    near_east = tuple((element[:VERTICAL_STRATA] for element in nearby))
    near_north = tuple((element[VERTICAL_STRATA : 2 * VERTICAL_STRATA] for element in nearby))
    near_tracer = tuple((element[2 * VERTICAL_STRATA : 3 * VERTICAL_STRATA] for element in nearby))
    near_depth = tuple((element[3 * VERTICAL_STRATA] for element in nearby))
    row_index = (lax.axis_index("lat") * lat_cells + jnp.arange(lat_cells)).astype(jnp.float32)
    rotation = rotation_rate(row_index, total_rows)[:, None]
    zonal_flow_guess, meridional_flow_guess, advected_scalar = baroclinic(
        layers,
        zonal_flow_middle,
        meridional_flow_middle,
        heat_content,
        column_depth_count,
        near_east,
        near_north,
        near_tracer,
        near_depth,
        rotation,
    )
    depth_means = jnp.stack(
        [
            jnp.sum(zonal_flow_guess, axis=0) * (1.0 / VERTICAL_STRATA),
            jnp.sum(meridional_flow_guess, axis=0) * (1.0 / VERTICAL_STRATA),
        ]
    )
    near_means = field_rim(depth_means)
    source = barotropic_source(
        tuple((element[0] for element in near_means)),
        tuple((element[1] for element in near_means)),
        column_depth_count,
        former_free_elevation,
    )
    grids_list = hierarchy(fine_coefficients(column_depth_count, near_depth))

    def coarse_solve(coeffs, coarse_source):
        return coarse_sweeps(coeffs, coarse_source, plane_near)

    pressure = None
    for cycle_number in range(CYCLES):
        pressure = multigrid_cycle(grids_list, 0, source, pressure, plane_near, coarse_solve)
    wet_cell = (layers < column_depth_count).astype(jnp.float32)
    zonal_new, meridional_new = corrected(
        wet_cell, zonal_flow_guess, meridional_flow_guess, plane_near(pressure)
    )
    return (zonal_new, meridional_new, advected_scalar, pressure)


def solution(mesh):
    placed = (
        P(None, "lat", "lon"),
        P(None, "lat", "lon"),
        P(None, "lat", "lon"),
        P("lat", "lon"),
        P("lat", "lon"),
    )
    return jax.shard_map(
        shards,
        mesh=mesh,
        in_specs=placed,
        out_specs=(
            P(None, "lat", "lon"),
            P(None, "lat", "lon"),
            P(None, "lat", "lon"),
            P("lat", "lon"),
        ),
        check_vma=False,
    )
```

profile of v0, /device:TPU:32, one launch (start us, length us, event | category | flops | bytes accessed | tf_op | source)
XLA Modules:
  0.0 829.3 jit_solution(6521523377938852642)
XLA Ops:
  2.8 13.7 %collective-permute-start.1 = (f32[25,32,1]{2,1,0:T(8,128)S(1)}, f32[25,32,1]{2,1,0:T(8,128)S(1)}, u32[]{:S(2)}, u32[]{:S(2)}) collective-permute-start(f32[25,32,1]{2,1,0:T(8,128)S(1)} %get-tuple-element.71), channel_id=1, source_target_pairs={{16,0},{32,16},{48,32},{64,48},{80,64},{96,80},{112,96},{128,112},... | collective-permute-start | bytes 9608 | tf_op jit(solution)/shard_map/ppermute | solution.py:29
  18.6 16.1 %collective-permute-done.1 = f32[25,32,1]{2,1,0:T(8,128)S(1)} collective-permute-done((f32[25,32,1]{2,1,0:T(8,128)S(1)}, f32[25,32,1]{2,1,0:T(8,128)S(1)}, u32[]{:S(2)}, u32[]{:S(2)}) %collective-permute-start.1) | collective-permute-done | bytes 3232 | tf_op jit(solution)/shard_map/ppermute | solution.py:29
  36.9 12.3 %collective-permute-start.3 = (f32[25,1,258]{2,1,0:T(1,128)S(1)}, f32[25,1,258]{2,1,0:T(1,128)S(1)}, u32[]{:S(2)}, u32[]{:S(2)}) collective-permute-start(f32[25,1,258]{2,1,0:T(1,128)S(1)} %get-tuple-element.65), channel_id=1, source_target_pairs={{1,0},{2,1},{3,2},{4,3},{5,4},{6,5},{7,6},{8,7},{9,8},{10,9},{11,1... | collective-permute-start | bytes 77408 | tf_op jit(solution)/shard_map/ppermute | solution.py:29
  60.9 8.8 %collective-permute-done.4 = f32[2,32,1]{2,1,0:T(8,128)S(1)} collective-permute-done((f32[2,32,1]{2,1,0:T(8,128)S(1)}, f32[2,32,1]{2,1,0:T(8,128)S(1)}, u32[]{:S(2)}, u32[]{:S(2)}) %collective-permute-start.4) | collective-permute-done | bytes 288 | tf_op jit(solution)/shard_map/ppermute | solution.py:26
  87.6 8.6 %collective-permute-done.8 = f32[32,1]{1,0:T(8,128)S(1)} collective-permute-done((f32[32,1]{1,0:T(8,128)S(1)}, f32[32,1]{1,0:T(8,128)S(1)}, u32[]{:S(2)}, u32[]{:S(2)}) %collective-permute-start.8) | collective-permute-done | bytes 160 | tf_op jit(solution)/shard_map/ppermute | solution.py:26
  113.3 8.6 %collective-permute-done.12 = f32[16,1]{1,0:T(8,128)S(1)} collective-permute-done((f32[16,1]{1,0:T(8,128)S(1)}, f32[16,1]{1,0:T(8,128)S(1)}, u32[]{:S(2)}, u32[]{:S(2)}) %collective-permute-start.12) | collective-permute-done | bytes 96 | tf_op jit(solution)/shard_map/ppermute | solution.py:26
  138.7 8.5 %collective-permute-done.16 = f32[8,1]{1,0:T(8,128)S(1)} collective-permute-done((f32[8,1]{1,0:T(8,128)S(1)}, f32[8,1]{1,0:T(8,128)S(1)}, u32[]{:S(2)}, u32[]{:S(2)}) %collective-permute-start.16) | collective-permute-done | bytes 64 | tf_op jit(solution)/shard_map/ppermute | solution.py:26
  164.8 8.5 %collective-permute-done.20 = f32[4,1]{1,0:T(4,128)S(1)} collective-permute-done((f32[4,1]{1,0:T(4,128)S(1)}, f32[4,1]{1,0:T(4,128)S(1)}, u32[]{:S(2)}, u32[]{:S(2)}) %collective-permute-start.20) | collective-permute-done | bytes 48 | tf_op jit(solution)/shard_map/ppermute | solution.py:26
  189.2 8.5 %collective-permute-done.24 = f32[4,1]{1,0:T(4,128)S(1)} collective-permute-done((f32[4,1]{1,0:T(4,128)S(1)}, f32[4,1]{1,0:T(4,128)S(1)}, u32[]{:S(2)}, u32[]{:S(2)}) %collective-permute-start.24) | collective-permute-done | bytes 48 | tf_op jit(solution)/shard_map/ppermute | solution.py:26
  213.6 8.5 %collective-permute-done.28 = f32[4,1]{1,0:T(4,128)S(1)} collective-permute-done((f32[4,1]{1,0:T(4,128)S(1)}, f32[4,1]{1,0:T(4,128)S(1)}, u32[]{:S(2)}, u32[]{:S(2)}) %collective-permute-start.28) | collective-permute-done | bytes 48 | tf_op jit(solution)/shard_map/ppermute | solution.py:26
  238.2 8.5 %collective-permute-done.32 = f32[8,1]{1,0:T(8,128)S(1)} collective-permute-done((f32[8,1]{1,0:T(8,128)S(1)}, f32[8,1]{1,0:T(8,128)S(1)}, u32[]{:S(2)}, u32[]{:S(2)}) %collective-permute-start.32) | collective-permute-done | bytes 64 | tf_op jit(solution)/shard_map/ppermute | solution.py:26
  262.9 8.6 %collective-permute-done.36 = f32[16,1]{1,0:T(8,128)S(1)} collective-permute-done((f32[16,1]{1,0:T(8,128)S(1)}, f32[16,1]{1,0:T(8,128)S(1)}, u32[]{:S(2)}, u32[]{:S(2)}) %collective-permute-start.36) | collective-permute-done | bytes 96 | tf_op jit(solution)/shard_map/ppermute | solution.py:26
  287.6 8.7 %collective-permute-done.40 = f32[32,1]{1,0:T(8,128)S(1)} collective-permute-done((f32[32,1]{1,0:T(8,128)S(1)}, f32[32,1]{1,0:T(8,128)S(1)}, u32[]{:S(2)}, u32[]{:S(2)}) %collective-permute-start.40) | collective-permute-done | bytes 160 | tf_op jit(solution)/shard_map/ppermute | solution.py:26
  312.3 8.7 %collective-permute-done.44 = f32[32,1]{1,0:T(8,128)S(1)} collective-permute-done((f32[32,1]{1,0:T(8,128)S(1)}, f32[32,1]{1,0:T(8,128)S(1)}, u32[]{:S(2)}, u32[]{:S(2)}) %collective-permute-start.44) | collective-permute-done | bytes 160 | tf_op jit(solution)/shard_map/ppermute | solution.py:26
  336.9 8.7 %collective-permute-done.48 = f32[32,1]{1,0:T(8,128)S(1)} collective-permute-done((f32[32,1]{1,0:T(8,128)S(1)}, f32[32,1]{1,0:T(8,128)S(1)}, u32[]{:S(2)}, u32[]{:S(2)}) %collective-permute-start.48) | collective-permute-done | bytes 160 | tf_op jit(solution)/shard_map/ppermute | solution.py:26
  362.3 8.6 %collective-permute-done.52 = f32[16,1]{1,0:T(8,128)S(1)} collective-permute-done((f32[16,1]{1,0:T(8,128)S(1)}, f32[16,1]{1,0:T(8,128)S(1)}, u32[]{:S(2)}, u32[]{:S(2)}) %collective-permute-start.52) | collective-permute-done | bytes 96 | tf_op jit(solution)/shard_map/ppermute | solution.py:26
  387.2 8.5 %collective-permute-done.56 = f32[8,1]{1,0:T(8,128)S(1)} collective-permute-done((f32[8,1]{1,0:T(8,128)S(1)}, f32[8,1]{1,0:T(8,128)S(1)}, u32[]{:S(2)}, u32[]{:S(2)}) %collective-permute-start.56) | collective-permute-done | bytes 64 | tf_op jit(solution)/shard_map/ppermute | solution.py:26
  411.9 8.5 %collective-permute-done.60 = f32[4,1]{1,0:T(4,128)S(1)} collective-permute-done((f32[4,1]{1,0:T(4,128)S(1)}, f32[4,1]{1,0:T(4,128)S(1)}, u32[]{:S(2)}, u32[]{:S(2)}) %collective-permute-start.60) | collective-permute-done | bytes 48 | tf_op jit(solution)/shard_map/ppermute | solution.py:26
  461.0 8.5 %collective-permute-done.68 = f32[4,1]{1,0:T(4,128)S(1)} collective-permute-done((f32[4,1]{1,0:T(4,128)S(1)}, f32[4,1]{1,0:T(4,128)S(1)}, u32[]{:S(2)}, u32[]{:S(2)}) %collective-permute-start.68) | collective-permute-done | bytes 48 | tf_op jit(solution)/shard_map/ppermute | solution.py:26
  485.6 8.5 %collective-permute-done.72 = f32[8,1]{1,0:T(8,128)S(1)} collective-permute-done((f32[8,1]{1,0:T(8,128)S(1)}, f32[8,1]{1,0:T(8,128)S(1)}, u32[]{:S(2)}, u32[]{:S(2)}) %collective-permute-start.72) | collective-permute-done | bytes 64 | tf_op jit(solution)/shard_map/ppermute | solution.py:26
  510.2 8.6 %collective-permute-done.76 = f32[16,1]{1,0:T(8,128)S(1)} collective-permute-done((f32[16,1]{1,0:T(8,128)S(1)}, f32[16,1]{1,0:T(8,128)S(1)}, u32[]{:S(2)}, u32[]{:S(2)}) %collective-permute-start.76) | collective-permute-done | bytes 96 | tf_op jit(solution)/shard_map/ppermute | solution.py:26
  535.0 8.7 %collective-permute-done.80 = f32[32,1]{1,0:T(8,128)S(1)} collective-permute-done((f32[32,1]{1,0:T(8,128)S(1)}, f32[32,1]{1,0:T(8,128)S(1)}, u32[]{:S(2)}, u32[]{:S(2)}) %collective-permute-start.80) | collective-permute-done | bytes 160 | tf_op jit(solution)/shard_map/ppermute | solution.py:26
  559.6 8.7 %collective-permute-done.84 = f32[32,1]{1,0:T(8,128)S(1)} collective-permute-done((f32[32,1]{1,0:T(8,128)S(1)}, f32[32,1]{1,0:T(8,128)S(1)}, u32[]{:S(2)}, u32[]{:S(2)}) %collective-permute-start.84) | collective-permute-done | bytes 160 | tf_op jit(solution)/shard_map/ppermute | solution.py:26
  584.3 8.7 %collective-permute-done.88 = f32[32,1]{1,0:T(8,128)S(1)} collective-permute-done((f32[32,1]{1,0:T(8,128)S(1)}, f32[32,1]{1,0:T(8,128)S(1)}, u32[]{:S(2)}, u32[]{:S(2)}) %collective-permute-start.88) | collective-permute-done | bytes 160 | tf_op jit(solution)/shard_map/ppermute | solution.py:26
  609.7 8.6 %collective-permute-done.92 = f32[16,1]{1,0:T(8,128)S(1)} collective-permute-done((f32[16,1]{1,0:T(8,128)S(1)}, f32[16,1]{1,0:T(8,128)S(1)}, u32[]{:S(2)}, u32[]{:S(2)}) %collective-permute-start.92) | collective-permute-done | bytes 96 | tf_op jit(solution)/shard_map/ppermute | solution.py:26
  634.5 8.5 %collective-permute-done.96 = f32[8,1]{1,0:T(8,128)S(1)} collective-permute-done((f32[8,1]{1,0:T(8,128)S(1)}, f32[8,1]{1,0:T(8,128)S(1)}, u32[]{:S(2)}, u32[]{:S(2)}) %collective-permute-start.96) | collective-permute-done | bytes 64 | tf_op jit(solution)/shard_map/ppermute | solution.py:26
  683.7 8.5 %collective-permute-done.104 = f32[4,1]{1,0:T(4,128)S(1)} collective-permute-done((f32[4,1]{1,0:T(4,128)S(1)}, f32[4,1]{1,0:T(4,128)S(1)}, u32[]{:S(2)}, u32[]{:S(2)}) %collective-permute-start.104) | collective-permute-done | bytes 48 | tf_op jit(solution)/shard_map/ppermute | solution.py:26
  708.1 8.5 %collective-permute-done.108 = f32[4,1]{1,0:T(4,128)S(1)} collective-permute-done((f32[4,1]{1,0:T(4,128)S(1)}, f32[4,1]{1,0:T(4,128)S(1)}, u32[]{:S(2)}, u32[]{:S(2)}) %collective-permute-start.108) | collective-permute-done | bytes 48 | tf_op jit(solution)/shard_map/ppermute | solution.py:26
  732.7 8.5 %collective-permute-done.112 = f32[8,1]{1,0:T(8,128)S(1)} collective-permute-done((f32[8,1]{1,0:T(8,128)S(1)}, f32[8,1]{1,0:T(8,128)S(1)}, u32[]{:S(2)}, u32[]{:S(2)}) %collective-permute-start.112) | collective-permute-done | bytes 64 | tf_op jit(solution)/shard_map/ppermute | solution.py:26
  757.4 8.6 %collective-permute-done.116 = f32[16,1]{1,0:T(8,128)S(1)} collective-permute-done((f32[16,1]{1,0:T(8,128)S(1)}, f32[16,1]{1,0:T(8,128)S(1)}, u32[]{:S(2)}, u32[]{:S(2)}) %collective-permute-start.116) | collective-permute-done | bytes 96 | tf_op jit(solution)/shard_map/ppermute | solution.py:26
  782.1 8.7 %collective-permute-done.120 = f32[32,1]{1,0:T(8,128)S(1)} collective-permute-done((f32[32,1]{1,0:T(8,128)S(1)}, f32[32,1]{1,0:T(8,128)S(1)}, u32[]{:S(2)}, u32[]{:S(2)}) %collective-permute-start.120) | collective-permute-done | bytes 160 | tf_op jit(solution)/shard_map/ppermute | solution.py:26
  806.8 8.7 %collective-permute-done.124 = f32[32,1]{1,0:T(8,128)S(1)} collective-permute-done((f32[32,1]{1,0:T(8,128)S(1)}, f32[32,1]{1,0:T(8,128)S(1)}, u32[]{:S(2)}, u32[]{:S(2)}) %collective-permute-start.124) | collective-permute-done | bytes 160 | tf_op jit(solution)/shard_map/ppermute | solution.py:26
  (514 shorter events, 535.8 us)
Async XLA Ops:
  2.8 31.8 %collective-permute-start.1 = (f32[25,32,1]{2,1,0:T(8,128)S(1)}, f32[25,32,1]{2,1,0:T(8,128)S(1)}, u32[]{:S(2)}, u32[]{:S(2)}) collective-permute-start(f32[25,32,1]{2,1,0:T(8,128)S(1)} %get-tuple-element.71), channel_id=1, source_target_pairs={{16,0},{32,16},{48,32},{64,48},{80,64},{96,80},{112,96},{128,112},... | collective-permute-start | bytes 9608 | tf_op jit(solution)/shard_map/ppermute | solution.py:29
  16.6 20.1 %collective-permute-start = (f32[25,32,1]{2,1,0:T(8,128)S(1)}, f32[25,32,1]{2,1,0:T(8,128)S(1)}, u32[]{:S(2)}, u32[]{:S(2)}) collective-permute-start(f32[25,32,1]{2,1,0:T(8,128)S(1)} %get-tuple-element.70), channel_id=1, source_target_pairs={{0,16},{16,32},{32,48},{48,64},{64,80},{80,96},{96,112},{112,128},... | collective-permute-start | bytes 9608 | tf_op jit(solution)/shard_map/ppermute | solution.py:26
  36.9 14.2 %collective-permute-start.3 = (f32[25,1,258]{2,1,0:T(1,128)S(1)}, f32[25,1,258]{2,1,0:T(1,128)S(1)}, u32[]{:S(2)}, u32[]{:S(2)}) collective-permute-start(f32[25,1,258]{2,1,0:T(1,128)S(1)} %get-tuple-element.65), channel_id=1, source_target_pairs={{1,0},{2,1},{3,2},{4,3},{5,4},{6,5},{7,6},{8,7},{9,8},{10,9},{11,1... | collective-permute-start | bytes 77408 | tf_op jit(solution)/shard_map/ppermute | solution.py:29
  58.5 11.3 %collective-permute-start.4 = (f32[2,32,1]{2,1,0:T(8,128)S(1)}, f32[2,32,1]{2,1,0:T(8,128)S(1)}, u32[]{:S(2)}, u32[]{:S(2)}) collective-permute-start(f32[2,32,1]{2,1,0:T(8,128)S(1)} %get-tuple-element.92), channel_id=1, source_target_pairs={{0,16},{16,32},{32,48},{48,64},{64,80},{80,96},{96,112},{112,128},... | collective-permute-start | bytes 776 | tf_op jit(solution)/shard_map/ppermute | solution.py:26
  85.1 11.1 %collective-permute-start.8 = (f32[32,1]{1,0:T(8,128)S(1)}, f32[32,1]{1,0:T(8,128)S(1)}, u32[]{:S(2)}, u32[]{:S(2)}) collective-permute-start(f32[32,1]{1,0:T(8,128)S(1)} %get-tuple-element.114), channel_id=1, source_target_pairs={{0,16},{16,32},{32,48},{48,64},{64,80},{80,96},{96,112},{112,128},... | collective-permute-start | bytes 392 | tf_op jit(solution)/shard_map/ppermute | solution.py:26
  110.9 11.0 %collective-permute-start.12 = (f32[16,1]{1,0:T(8,128)S(1)}, f32[16,1]{1,0:T(8,128)S(1)}, u32[]{:S(2)}, u32[]{:S(2)}) collective-permute-start(f32[16,1]{1,0:T(8,128)S(1)} %get-tuple-element.140), channel_id=1, source_target_pairs={{0,16},{16,32},{32,48},{48,64},{64,80},{80,96},{96,112},{112,128},... | collective-permute-start | bytes 200 | tf_op jit(solution)/shard_map/ppermute | solution.py:26
  136.3 10.9 %collective-permute-start.16 = (f32[8,1]{1,0:T(8,128)S(1)}, f32[8,1]{1,0:T(8,128)S(1)}, u32[]{:S(2)}, u32[]{:S(2)}) collective-permute-start(f32[8,1]{1,0:T(8,128)S(1)} %get-tuple-element.164), channel_id=1, source_target_pairs={{0,16},{16,32},{32,48},{48,64},{64,80},{80,96},{96,112},{112,128},... | collective-permute-start | bytes 104 | tf_op jit(solution)/shard_map/ppermute | solution.py:26
  162.3 10.9 %collective-permute-start.20 = (f32[4,1]{1,0:T(4,128)S(1)}, f32[4,1]{1,0:T(4,128)S(1)}, u32[]{:S(2)}, u32[]{:S(2)}) collective-permute-start(f32[4,1]{1,0:T(4,128)S(1)} %get-tuple-element.200), channel_id=1, source_target_pairs={{0,16},{16,32},{32,48},{48,64},{64,80},{80,96},{96,112},{112,128},... | collective-permute-start | bytes 56 | tf_op jit(solution)/shard_map/ppermute | solution.py:26
  186.8 10.9 %collective-permute-start.24 = (f32[4,1]{1,0:T(4,128)S(1)}, f32[4,1]{1,0:T(4,128)S(1)}, u32[]{:S(2)}, u32[]{:S(2)}) collective-permute-start(f32[4,1]{1,0:T(4,128)S(1)} %get-tuple-element.196), channel_id=1, source_target_pairs={{0,16},{16,32},{32,48},{48,64},{64,80},{80,96},{96,112},{112,128},... | collective-permute-start | bytes 56 | tf_op jit(solution)/shard_map/ppermute | solution.py:26
  235.8 10.9 %collective-permute-start.32 = (f32[8,1]{1,0:T(8,128)S(1)}, f32[8,1]{1,0:T(8,128)S(1)}, u32[]{:S(2)}, u32[]{:S(2)}) collective-permute-start(f32[8,1]{1,0:T(8,128)S(1)} %get-tuple-element.160), channel_id=1, source_target_pairs={{0,16},{16,32},{32,48},{48,64},{64,80},{80,96},{96,112},{112,128},... | collective-permute-start | bytes 104 | tf_op jit(solution)/shard_map/ppermute | solution.py:26
  260.4 11.0 %collective-permute-start.36 = (f32[16,1]{1,0:T(8,128)S(1)}, f32[16,1]{1,0:T(8,128)S(1)}, u32[]{:S(2)}, u32[]{:S(2)}) collective-permute-start(f32[16,1]{1,0:T(8,128)S(1)} %get-tuple-element.138), channel_id=1, source_target_pairs={{0,16},{16,32},{32,48},{48,64},{64,80},{80,96},{96,112},{112,128},... | collective-permute-start | bytes 200 | tf_op jit(solution)/shard_map/ppermute | solution.py:26
  285.2 11.1 %collective-permute-start.40 = (f32[32,1]{1,0:T(8,128)S(1)}, f32[32,1]{1,0:T(8,128)S(1)}, u32[]{:S(2)}, u32[]{:S(2)}) collective-permute-start(f32[32,1]{1,0:T(8,128)S(1)} %get-tuple-element.112), channel_id=1, source_target_pairs={{0,16},{16,32},{32,48},{48,64},{64,80},{80,96},{96,112},{112,128},... | collective-permute-start | bytes 392 | tf_op jit(solution)/shard_map/ppermute | solution.py:26
  309.9 11.1 %collective-permute-start.44 = (f32[32,1]{1,0:T(8,128)S(1)}, f32[32,1]{1,0:T(8,128)S(1)}, u32[]{:S(2)}, u32[]{:S(2)}) collective-permute-start(f32[32,1]{1,0:T(8,128)S(1)} %get-tuple-element.110), channel_id=1, source_target_pairs={{0,16},{16,32},{32,48},{48,64},{64,80},{80,96},{96,112},{112,128},... | collective-permute-start | bytes 392 | tf_op jit(solution)/shard_map/ppermute | solution.py:26
  334.5 11.1 %collective-permute-start.48 = (f32[32,1]{1,0:T(8,128)S(1)}, f32[32,1]{1,0:T(8,128)S(1)}, u32[]{:S(2)}, u32[]{:S(2)}) collective-permute-start(f32[32,1]{1,0:T(8,128)S(1)} %get-tuple-element.108), channel_id=1, source_target_pairs={{0,16},{16,32},{32,48},{48,64},{64,80},{80,96},{96,112},{112,128},... | collective-permute-start | bytes 392 | tf_op jit(solution)/shard_map/ppermute | solution.py:26
  359.9 11.0 %collective-permute-start.52 = (f32[16,1]{1,0:T(8,128)S(1)}, f32[16,1]{1,0:T(8,128)S(1)}, u32[]{:S(2)}, u32[]{:S(2)}) collective-permute-start(f32[16,1]{1,0:T(8,128)S(1)} %get-tuple-element.136), channel_id=1, source_target_pairs={{0,16},{16,32},{32,48},{48,64},{64,80},{80,96},{96,112},{112,128},... | collective-permute-start | bytes 200 | tf_op jit(solution)/shard_map/ppermute | solution.py:26
  384.7 10.9 %collective-permute-start.56 = (f32[8,1]{1,0:T(8,128)S(1)}, f32[8,1]{1,0:T(8,128)S(1)}, u32[]{:S(2)}, u32[]{:S(2)}) collective-permute-start(f32[8,1]{1,0:T(8,128)S(1)} %get-tuple-element.156), channel_id=1, source_target_pairs={{0,16},{16,32},{32,48},{48,64},{64,80},{80,96},{96,112},{112,128},... | collective-permute-start | bytes 104 | tf_op jit(solution)/shard_map/ppermute | solution.py:26
  409.5 10.9 %collective-permute-start.60 = (f32[4,1]{1,0:T(4,128)S(1)}, f32[4,1]{1,0:T(4,128)S(1)}, u32[]{:S(2)}, u32[]{:S(2)}) collective-permute-start(f32[4,1]{1,0:T(4,128)S(1)} %get-tuple-element.188), channel_id=1, source_target_pairs={{0,16},{16,32},{32,48},{48,64},{64,80},{80,96},{96,112},{112,128},... | collective-permute-start | bytes 56 | tf_op jit(solution)/shard_map/ppermute | solution.py:26
  433.9 11.1 %collective-permute-start.64 = (f32[4,1]{1,0:T(4,128)S(1)}, f32[4,1]{1,0:T(4,128)S(1)}, u32[]{:S(2)}, u32[]{:S(2)}) collective-permute-start(f32[4,1]{1,0:T(4,128)S(1)} %get-tuple-element.184), channel_id=1, source_target_pairs={{0,16},{16,32},{32,48},{48,64},{64,80},{80,96},{96,112},{112,128},... | collective-permute-start | bytes 56 | tf_op jit(solution)/shard_map/ppermute | solution.py:26
  458.5 10.9 %collective-permute-start.68 = (f32[4,1]{1,0:T(4,128)S(1)}, f32[4,1]{1,0:T(4,128)S(1)}, u32[]{:S(2)}, u32[]{:S(2)}) collective-permute-start(f32[4,1]{1,0:T(4,128)S(1)} %get-tuple-element.180), channel_id=1, source_target_pairs={{0,16},{16,32},{32,48},{48,64},{64,80},{80,96},{96,112},{112,128},... | collective-permute-start | bytes 56 | tf_op jit(solution)/shard_map/ppermute | solution.py:26
  483.1 10.9 %collective-permute-start.72 = (f32[8,1]{1,0:T(8,128)S(1)}, f32[8,1]{1,0:T(8,128)S(1)}, u32[]{:S(2)}, u32[]{:S(2)}) collective-permute-start(f32[8,1]{1,0:T(8,128)S(1)} %get-tuple-element.152), channel_id=1, source_target_pairs={{0,16},{16,32},{32,48},{48,64},{64,80},{80,96},{96,112},{112,128},... | collective-permute-start | bytes 104 | tf_op jit(solution)/shard_map/ppermute | solution.py:26
  507.8 11.0 %collective-permute-start.76 = (f32[16,1]{1,0:T(8,128)S(1)}, f32[16,1]{1,0:T(8,128)S(1)}, u32[]{:S(2)}, u32[]{:S(2)}) collective-permute-start(f32[16,1]{1,0:T(8,128)S(1)} %get-tuple-element.134), channel_id=1, source_target_pairs={{0,16},{16,32},{32,48},{48,64},{64,80},{80,96},{96,112},{112,128},... | collective-permute-start | bytes 200 | tf_op jit(solution)/shard_map/ppermute | solution.py:26
  532.6 11.1 %collective-permute-start.80 = (f32[32,1]{1,0:T(8,128)S(1)}, f32[32,1]{1,0:T(8,128)S(1)}, u32[]{:S(2)}, u32[]{:S(2)}) collective-permute-start(f32[32,1]{1,0:T(8,128)S(1)} %get-tuple-element.106), channel_id=1, source_target_pairs={{0,16},{16,32},{32,48},{48,64},{64,80},{80,96},{96,112},{112,128},... | collective-permute-start | bytes 392 | tf_op jit(solution)/shard_map/ppermute | solution.py:26
  557.2 11.1 %collective-permute-start.84 = (f32[32,1]{1,0:T(8,128)S(1)}, f32[32,1]{1,0:T(8,128)S(1)}, u32[]{:S(2)}, u32[]{:S(2)}) collective-permute-start(f32[32,1]{1,0:T(8,128)S(1)} %get-tuple-element.104), channel_id=1, source_target_pairs={{0,16},{16,32},{32,48},{48,64},{64,80},{80,96},{96,112},{112,128},... | collective-permute-start | bytes 392 | tf_op jit(solution)/shard_map/ppermute | solution.py:26
  581.9 11.1 %collective-permute-start.88 = (f32[32,1]{1,0:T(8,128)S(1)}, f32[32,1]{1,0:T(8,128)S(1)}, u32[]{:S(2)}, u32[]{:S(2)}) collective-permute-start(f32[32,1]{1,0:T(8,128)S(1)} %get-tuple-element.102), channel_id=1, source_target_pairs={{0,16},{16,32},{32,48},{48,64},{64,80},{80,96},{96,112},{112,128},... | collective-permute-start | bytes 392 | tf_op jit(solution)/shard_map/ppermute | solution.py:26
  607.2 11.0 %collective-permute-start.92 = (f32[16,1]{1,0:T(8,128)S(1)}, f32[16,1]{1,0:T(8,128)S(1)}, u32[]{:S(2)}, u32[]{:S(2)}) collective-permute-start(f32[16,1]{1,0:T(8,128)S(1)} %get-tuple-element.132), channel_id=1, source_target_pairs={{0,16},{16,32},{32,48},{48,64},{64,80},{80,96},{96,112},{112,128},... | collective-permute-start | bytes 200 | tf_op jit(solution)/shard_map/ppermute | solution.py:26
  632.1 10.9 %collective-permute-start.96 = (f32[8,1]{1,0:T(8,128)S(1)}, f32[8,1]{1,0:T(8,128)S(1)}, u32[]{:S(2)}, u32[]{:S(2)}) collective-permute-start(f32[8,1]{1,0:T(8,128)S(1)} %get-tuple-element.148), channel_id=1, source_target_pairs={{0,16},{16,32},{32,48},{48,64},{64,80},{80,96},{96,112},{112,128},... | collective-permute-start | bytes 104 | tf_op jit(solution)/shard_map/ppermute | solution.py:26
  681.3 10.9 %collective-permute-start.104 = (f32[4,1]{1,0:T(4,128)S(1)}, f32[4,1]{1,0:T(4,128)S(1)}, u32[]{:S(2)}, u32[]{:S(2)}) collective-permute-start(f32[4,1]{1,0:T(4,128)S(1)} %get-tuple-element.172), channel_id=1, source_target_pairs={{0,16},{16,32},{32,48},{48,64},{64,80},{80,96},{96,112},{112,128},... | collective-permute-start | bytes 56 | tf_op jit(solution)/shard_map/ppermute | solution.py:26
  705.7 10.9 %collective-permute-start.108 = (f32[4,1]{1,0:T(4,128)S(1)}, f32[4,1]{1,0:T(4,128)S(1)}, u32[]{:S(2)}, u32[]{:S(2)}) collective-permute-start(f32[4,1]{1,0:T(4,128)S(1)} %get-tuple-element.168), channel_id=1, source_target_pairs={{0,16},{16,32},{32,48},{48,64},{64,80},{80,96},{96,112},{112,128},... | collective-permute-start | bytes 56 | tf_op jit(solution)/shard_map/ppermute | solution.py:26
  730.3 10.9 %collective-permute-start.112 = (f32[8,1]{1,0:T(8,128)S(1)}, f32[8,1]{1,0:T(8,128)S(1)}, u32[]{:S(2)}, u32[]{:S(2)}) collective-permute-start(f32[8,1]{1,0:T(8,128)S(1)} %get-tuple-element.144), channel_id=1, source_target_pairs={{0,16},{16,32},{32,48},{48,64},{64,80},{80,96},{96,112},{112,128},... | collective-permute-start | bytes 104 | tf_op jit(solution)/shard_map/ppermute | solution.py:26
  754.9 11.0 %collective-permute-start.116 = (f32[16,1]{1,0:T(8,128)S(1)}, f32[16,1]{1,0:T(8,128)S(1)}, u32[]{:S(2)}, u32[]{:S(2)}) collective-permute-start(f32[16,1]{1,0:T(8,128)S(1)} %get-tuple-element.130), channel_id=1, source_target_pairs={{0,16},{16,32},{32,48},{48,64},{64,80},{80,96},{96,112},{112,128},... | collective-permute-start | bytes 200 | tf_op jit(solution)/shard_map/ppermute | solution.py:26
  779.7 11.1 %collective-permute-start.120 = (f32[32,1]{1,0:T(8,128)S(1)}, f32[32,1]{1,0:T(8,128)S(1)}, u32[]{:S(2)}, u32[]{:S(2)}) collective-permute-start(f32[32,1]{1,0:T(8,128)S(1)} %get-tuple-element.100), channel_id=1, source_target_pairs={{0,16},{16,32},{32,48},{48,64},{64,80},{80,96},{96,112},{112,128},... | collective-permute-start | bytes 392 | tf_op jit(solution)/shard_map/ppermute | solution.py:26
  804.4 11.1 %collective-permute-start.124 = (f32[32,1]{1,0:T(8,128)S(1)}, f32[32,1]{1,0:T(8,128)S(1)}, u32[]{:S(2)}, u32[]{:S(2)}) collective-permute-start(f32[32,1]{1,0:T(8,128)S(1)} %get-tuple-element.98), channel_id=1, source_target_pairs={{0,16},{16,32},{32,48},{48,64},{64,80},{80,96},{96,112},{112,128},... | collective-permute-start | bytes 392 | tf_op jit(solution)/shard_map/ppermute | solution.py:26
  (102 other events, 765.9 us)
where the time goes:
time: 833 us; the launch traced here: 829 us
  starting transfers between devices  407 us (49%)
  waiting for transfers between devices  393 us (47%)
  other arithmetic  13.9 us (2%)
  local copies, waits for them, and re-layouts  13 us (2%)
    ppermute x64, waiting for transfers between devices, with_halo(): lax.ppermute(lax.slice_in_dim(block, block.shape[dim] - width, None, axis...  376 us
    ppermute x64, starting transfers between devices, with_halo(): lax.ppermute(lax.slice_in_dim(block, 0, width, axis=dim), axis, backward)  269 us
    ppermute x64, starting transfers between devices, with_halo(): lax.ppermute(lax.slice_in_dim(block, block.shape[dim] - width, None, axis...  138 us
  transfers between devices with their start and end apart: 128, of which 65 were waited for; matrix products, arithmetic and copies ran while one was open for 0% of the time, Pallas kernels for 0%

commit v1 on v0

v1 whole, which is shorter than its diff:
```python
import functools

import jax
import jax.numpy as jnp
from jax import lax
from jax.experimental import pallas as pl
from jax.experimental.pallas import tpu as pltpu
from jax.sharding import PartitionSpec as P

LEVELS = 8
CYCLES = 3
SWEEPS = 4
TIME_STEP = 0.2
VISCOSITY = 1.0
DIFFUSIVITY = 1.0
CORIOLIS = 1.0
MASS_TERM = 0.05
GRAVITY_STEP = 0.5

ROWS = 32
COLS = 256
LANES = 128
WIDE = 512
MESH_IDS = pl.DeviceIdType.MESH

CLASSES = (4, 2, 1, 1)
STEP = (1, 1, 1, 2)
ORIGIN = (72, 40, 24, 16)
HEIGHT = (176, 96, 56, 40)
MASS = tuple(MASS_TERM * 4.0**g for g in range(4))

LAT_MOVES = (1, -1, 2, -2)


def east_of(parts, step):
    turned = pltpu.roll(parts[0], LANES - step, 1)
    return list(parts[1:]) + [turned]


def west_of(parts, step):
    turned = pltpu.roll(parts[-1], step, 1)
    return [turned] + list(parts[:-1])


def each_chunk(first, last, body, unroll=5):
    count = (last - first) // 8
    if count <= unroll:
        for i in range(count):
            body(first + 8 * i)
        return
    while count % unroll:
        unroll -= 1

    def step(i, carry):
        for j in range(unroll):
            body(pl.multiple_of(first + (i * unroll + j) * 8, 8))
        return carry

    lax.fori_loop(0, count // unroll, step, 0)


def split_three(values):
    high = values.astype(jnp.bfloat16)
    rest = values - high.astype(jnp.float32)
    middle = rest.astype(jnp.bfloat16)
    low = (rest - middle.astype(jnp.float32)).astype(jnp.bfloat16)
    return jnp.concatenate([high, middle, low], axis=0)


def exact_select(values, choice):
    count = values.shape[0]
    product = jnp.dot(split_three(values), choice, preferred_element_type=jnp.float32)
    return (product[:count] + product[count : 2 * count]) + product[2 * count :]


def kernel(
    lon_count,
    lat_count,
    u_ref,
    v_ref,
    t_ref,
    depth_ref,
    elevation_ref,
    u_out,
    v_out,
    t_out,
    p_out,
    u_star,
    v_star,
    rows_send,
    rows_got,
    cols_send,
    cols_got,
    mean_send,
    mean_got,
    deep_send,
    deep_got,
    source_send,
    source_got,
    coarse_send,
    coarse_got,
    choice,
    unchoice,
    deep,
    grid_b,
    grid_p,
    grid_q,
    grid_we,
    grid_ww,
    grid_wn,
    grid_dg,
    grid_iv,
    grid_r,
    send_sem,
    recv_sem,
):
    lon = lax.axis_index("lon")
    lat = lax.axis_index("lat")
    sems = iter(range(64))

    def there(lon_move, lat_move):
        return {
            "lon": lax.rem(lon + lon_move + lon_count, lon_count),
            "lat": lax.rem(lat + lat_move + lat_count, lat_count),
        }

    def send(source, target, lon_move, lat_move):
        at = next(sems)
        return pltpu.make_async_remote_copy(
            src_ref=source,
            dst_ref=target,
            send_sem=send_sem.at[at],
            recv_sem=recv_sem.at[at],
            device_id=there(lon_move, lat_move),
            device_id_type=MESH_IDS,
        )

    def inside(lat_move):
        spot = lat + lat_move
        return jnp.where((spot >= 0) & (spot < lat_count), 1.0, 0.0).astype(jnp.float32)

    started = []

    def launch(copies):
        for copy in copies:
            copy.start()
        started.extend(copies)

    barrier = pltpu.get_barrier_semaphore()
    for lon_move, lat_move in [(1, 0), (-1, 0)] + [(0, m) for m in LAT_MOVES]:
        pl.semaphore_signal(
            barrier, inc=1, device_id=there(lon_move, lat_move), device_id_type=MESH_IDS
        )

    depth = depth_ref[...].astype(jnp.float32)
    lane8 = lax.broadcasted_iota(jnp.int32, (8, LANES), 1)
    fields = (u_ref, v_ref, t_ref)
    for side, row in ((0, ROWS - 1), (1, 0)):
        for f, field in enumerate(fields):
            for k in range(LEVELS):
                rows_send[side, 8 * f + k : 8 * f + k + 1, :] = field[
                    k * ROWS + row : k * ROWS + row + 1, :
                ]
        rows_send[side, pl.ds(24, 8), :] = jnp.broadcast_to(depth[row : row + 1, :], (8, COLS))

    def pack(i, carry):
        at_last, at_first = carry
        rows = pl.ds(pl.multiple_of(8 * i, 8), 8)
        for f, field in enumerate(fields):
            here = lane8 == i + 32 * f
            at_last = jnp.where(here, field[rows, COLS - 1 : COLS], at_last)
            at_first = jnp.where(here, field[rows, 0:1], at_first)
        return at_last, at_first

    zero8 = jnp.zeros((8, LANES), jnp.float32)
    at_last, at_first = lax.fori_loop(0, 32, pack, (zero8, zero8), unroll=4)
    elevation = elevation_ref[...]
    for side, edge, tile in ((0, at_last, 1), (1, at_first, 0)):
        cut = slice(tile * LANES, (tile + 1) * LANES)
        cols_send[side, 0:32, :] = depth[:, cut]
        cols_send[side, 32:64, :] = elevation[:, cut]
        cols_send[side, 64:72, :] = edge

    pl.semaphore_wait(barrier, 2 + len(LAT_MOVES))
    first = [
        send(cols_send.at[0], cols_got.at[0], 1, 0),
        send(cols_send.at[1], cols_got.at[1], -1, 0),
        send(rows_send.at[0], rows_got.at[0], 0, 1),
        send(rows_send.at[1], rows_got.at[1], 0, -1),
    ]
    launch(first)

    def order(n):
        return ((((n & 127) + 32) & 127) << 2) + (n >> 7)

    wanted = order(lax.broadcasted_iota(jnp.int32, (1, WIDE), 1))

    def fill(i, carry):
        rows = pl.ds(pl.multiple_of(32 * i, 32), 32)
        k = lax.broadcasted_iota(jnp.int32, (32, WIDE), 0) + 32 * i
        choice[rows, :] = jnp.where(k == wanted, 1.0, 0.0).astype(jnp.bfloat16)
        n = lax.broadcasted_iota(jnp.int32, (32, COLS), 0) + 32 * i
        column = lax.broadcasted_iota(jnp.int32, (32, COLS), 1) + LANES
        unchoice[rows, :] = jnp.where(order(n) == column, 1.0, 0.0).astype(jnp.bfloat16)
        return carry

    lax.fori_loop(0, WIDE // 32, fill, 0)
    for ref in list(grid_p) + list(grid_q) + list(grid_b) + list(grid_wn) + [deep]:
        ref[...] = jnp.zeros_like(ref)
    row_number = lax.broadcasted_iota(jnp.int32, (ROWS, LANES), 0)
    place = (lat * ROWS + row_number).astype(jnp.float32)
    angle = jnp.pi * ((place + 0.5) / (ROWS * lat_count) - 0.5)
    turning = CORIOLIS * jnp.sin(angle)
    rotation = jnp.concatenate([turning, turning], axis=1)

    for copy in first:
        copy.wait_recv()

    west_tile, east_tile = cols_got.at[0], cols_got.at[1]
    depth_wide = jnp.concatenate([west_tile[0:32, :], depth, east_tile[0:32, :]], axis=1)
    by_class = jnp.dot(
        depth_wide.astype(jnp.bfloat16), choice[...], preferred_element_type=jnp.float32
    )
    for c in range(4):
        deep_send[32 * c : 32 * c + 32, :] = by_class[:, LANES * c : LANES * (c + 1)]
    depth_copies = [
        send(deep_send, deep_got.at[i], 0, move) for i, move in enumerate(LAT_MOVES)
    ]
    launch(depth_copies)

    row = lax.broadcasted_iota(jnp.int32, (ROWS, COLS), 0)
    column = lax.broadcasted_iota(jnp.int32, (ROWS, COLS), 1)
    on_east, on_west = column == COLS - 1, column == 0
    on_north, on_south = row == ROWS - 1, row == 0

    def beside(values, east_edge, west_edge, north_edge, south_edge):
        return (
            jnp.where(on_east, east_edge, pltpu.roll(values, COLS - 1, 1)),
            jnp.where(on_west, west_edge, pltpu.roll(values, 1, 1)),
            jnp.where(on_north, north_edge, pltpu.roll(values, ROWS - 1, 0)),
            jnp.where(on_south, south_edge, pltpu.roll(values, 1, 0)),
        )

    depth_near = beside(
        depth,
        east_tile[0:32, 0:1],
        west_tile[0:32, LANES - 1 : LANES],
        rows_got[1, 24:25, :] * inside(1),
        rows_got[0, 24:25, :] * inside(-1),
    )
    open_depth = [jnp.minimum(depth, near) for near in depth_near]
    east_edges = east_tile[64:72, :]
    west_edges = west_tile[64:72, :]

    def near_field(f, field, k):
        values = field[pl.ds(pl.multiple_of(k * ROWS, ROWS), ROWS), :]
        turn = lax.rem(2 * LANES - 32 * f - 4 * k, LANES)
        east_lanes = pltpu.roll(east_edges, turn, 1)
        west_lanes = pltpu.roll(west_edges, turn, 1)
        east_edge = jnp.concatenate([east_lanes[:, g : g + 1] for g in range(4)], axis=0)
        west_edge = jnp.concatenate([west_lanes[:, g : g + 1] for g in range(4)], axis=0)
        north_edge = rows_got[1, pl.ds(8 * f + k, 1), :]
        south_edge = rows_got[0, pl.ds(8 * f + k, 1), :]
        return values, beside(values, east_edge, west_edge, north_edge, south_edge)

    def laplace(faces, values, nearby):
        terms = [jnp.where(face, near - values, 0.0) for face, near in zip(faces, nearby)]
        return (terms[0] + terms[1]) + (terms[2] + terms[3])

    def momentum(k, carry):
        sum_u, sum_v = carry
        level = k.astype(jnp.float32)
        faces = [level < limit for limit in open_depth]
        wet = level < depth
        u, near_u = near_field(0, u_ref, k)
        v, near_v = near_field(1, v_ref, k)
        guess_u = u + TIME_STEP * (VISCOSITY * laplace(faces, u, near_u) + rotation * v)
        guess_v = v + TIME_STEP * (VISCOSITY * laplace(faces, v, near_v) - rotation * u)
        guess_u = jnp.where(wet, guess_u, 0.0)
        guess_v = jnp.where(wet, guess_v, 0.0)
        rows = pl.ds(pl.multiple_of(k * ROWS, ROWS), ROWS)
        u_star[rows, :] = guess_u
        v_star[rows, :] = guess_v
        return sum_u + guess_u, sum_v + guess_v

    zero = jnp.zeros((ROWS, COLS), jnp.float32)
    sum_u, sum_v = lax.fori_loop(0, LEVELS, momentum, (zero, zero))
    mean_u = sum_u * (1.0 / LEVELS)
    mean_v = sum_v * (1.0 / LEVELS)
    for side, tile in ((0, 1), (1, 0)):
        cut = slice(tile * LANES, (tile + 1) * LANES)
        mean_send[side, 0:32, :] = mean_u[:, cut]
        mean_send[side, 32:64, :] = mean_v[:, cut]
    mean_copies = [
        send(mean_send.at[0], mean_got.at[0], 1, 0),
        send(mean_send.at[1], mean_got.at[1], -1, 0),
    ]
    launch(mean_copies)

    def tracer(k, carry):
        level = k.astype(jnp.float32)
        faces = [level < limit for limit in open_depth]
        t, near_t = near_field(2, t_ref, k)
        u, near_u = near_field(0, u_ref, k)
        v, near_v = near_field(1, v_ref, k)
        spread = laplace(faces, t, near_t)
        east = jnp.where(faces[0], (u + near_u[0]) * 0.5, 0.0)
        west = jnp.where(faces[1], (near_u[1] + u) * 0.5, 0.0)
        north = jnp.where(faces[2], (v + near_v[2]) * 0.5, 0.0)
        south = jnp.where(faces[3], (near_v[3] + v) * 0.5, 0.0)
        transport = (east * (t + near_t[0]) - west * (near_t[1] + t)) + (
            north * (t + near_t[2]) - south * (near_t[3] + t)
        )
        result = t + TIME_STEP * (DIFFUSIVITY * spread - 0.5 * transport)
        rows = pl.ds(pl.multiple_of(k * ROWS, ROWS), ROWS)
        t_out[rows, :] = jnp.where(level < depth, result, 0.0)
        return carry

    lax.fori_loop(0, LEVELS, tracer, 0)

    for copy in mean_copies:
        copy.wait_recv()
    west_mean, east_mean = mean_got.at[0], mean_got.at[1]
    wide_u = jnp.concatenate([west_mean[0:32, :], mean_u, east_mean[0:32, :]], axis=1)
    wide_v = jnp.concatenate([west_mean[32:64, :], mean_v, east_mean[32:64, :]], axis=1)
    wide_eta = jnp.concatenate([west_tile[32:64, :], elevation, east_tile[32:64, :]], axis=1)
    wide_row = lax.broadcasted_iota(jnp.int32, (ROWS, WIDE), 0)
    north_v = jnp.where(wide_row == ROWS - 1, 0.0, pltpu.roll(wide_v, ROWS - 1, 0))
    south_v = jnp.where(wide_row == 0, 0.0, pltpu.roll(wide_v, 1, 0))
    across = pltpu.roll(wide_u, WIDE - 1, 1) - pltpu.roll(wide_u, 1, 1)
    source = jnp.where(
        depth_wide > 0.5, wide_eta - 0.5 * (across + (north_v - south_v)), 0.0
    )
    ends = jnp.where(
        lax.broadcasted_iota(jnp.int32, (16, WIDE), 0) == 0, wide_v[0:1, :], wide_v[31:32, :]
    )
    by_class = exact_select(jnp.concatenate([source, ends], axis=0), choice[...])
    for c in range(4):
        cut = slice(LANES * c, LANES * (c + 1))
        source_send[32 * c : 32 * c + 32, :] = by_class[0:32, cut]
        source_send[128 + c : 129 + c, :] = by_class[32:33, cut]
        source_send[132 + c : 133 + c, :] = by_class[33:34, cut]
    source_copies = [
        send(source_send, source_got.at[i], 0, move) for i, move in enumerate(LAT_MOVES)
    ]
    launch(source_copies)

    for copy in depth_copies:
        copy.wait_recv()

    def slot_of(lat_move):
        return LAT_MOVES.index(-lat_move)

    for move in range(-2, 3):
        for c in range(4):
            rows = pl.ds(ORIGIN[0] + 32 * move, 32)
            if move == 0:
                deep[c, rows, :] = deep_send[32 * c : 32 * c + 32, :]
            else:
                deep[c, rows, :] = (
                    deep_got[slot_of(move), 32 * c : 32 * c + 32, :] * inside(move)
                )

    def finish_weights(g, rows):
        we = [grid_we[g][c, rows, :] for c in range(CLASSES[g])]
        ww = west_of(we, STEP[g])
        grid_ww[g][rows, :] = ww[0]
        before = pl.ds(rows.start - 1, 8)
        for c in range(CLASSES[g]):
            near = (we[c] + ww[c]) + (grid_wn[g][c, rows, :] + grid_wn[g][c, before, :])
            grid_dg[g][c, rows, :] = MASS[g] + near
            grid_iv[g][c, rows, :] = 1.0 / (MASS[g] + 2.0 * near)

    def fine_weights(at):
        rows, after = pl.ds(at, 8), pl.ds(at + 1, 8)
        columns = [deep[c, rows, :] * (1.0 / LEVELS) for c in range(4)]
        for c, near in enumerate(east_of(columns, 1)):
            grid_we[0][c, rows, :] = jnp.minimum(columns[c], near)
            north = deep[c, after, :] * (1.0 / LEVELS)
            grid_wn[0][c, rows, :] = jnp.minimum(columns[c], north)

    def whole(g):
        return ORIGIN[g] - (64 >> g), ORIGIN[g] + ((96 >> g) + 7) // 8 * 8

    def pair_lanes(values):
        even = (lax.broadcasted_iota(jnp.int32, values.shape, 1) & 1) == 0
        return even, pltpu.roll(values, LANES - 1, 1), pltpu.roll(values, 1, 1)

    def finer_rows(g, at):
        return 2 * (at - ORIGIN[g]) + ORIGIN[g - 1]

    each_chunk(*whole(0), fine_weights)
    each_chunk(*whole(0), lambda at: finish_weights(0, pl.ds(at, 8)))
    for g in (1, 2, 3):

        def coarse_weights(at, g=g):
            rows = pl.ds(at, 8)
            above = finer_rows(g, at)
            even_rows, odd_rows = pl.ds(above, 8, stride=2), pl.ds(above + 1, 8, stride=2)
            finer_we, finer_wn = grid_we[g - 1], grid_wn[g - 1]
            if g < 3:
                for c in range(CLASSES[g]):
                    grid_we[g][c, rows, :] = (
                        finer_we[2 * c + 1, even_rows, :] + finer_we[2 * c + 1, odd_rows, :]
                    )
                    grid_wn[g][c, rows, :] = (
                        finer_wn[2 * c, odd_rows, :] + finer_wn[2 * c + 1, odd_rows, :]
                    )
            else:
                we = finer_we[0, even_rows, :] + finer_we[0, odd_rows, :]
                even, east, west = pair_lanes(we)
                grid_we[g][0, rows, :] = jnp.where(even, east, we)
                wn = finer_wn[0, odd_rows, :]
                even, east, west = pair_lanes(wn)
                grid_wn[g][0, rows, :] = wn + jnp.where(even, east, west)

        each_chunk(*whole(g), coarse_weights)
        each_chunk(*whole(g), lambda at, g=g: finish_weights(g, pl.ds(at, 8)))

    for copy in source_copies:
        copy.wait_recv()

    def arrived(move):
        return source_send if move == 0 else source_got.at[slot_of(move)]

    rows32 = lax.broadcasted_iota(jnp.int32, (ROWS, LANES), 0)
    for move in range(-2, 3):
        block = arrived(move)
        for c in range(4):
            rows = pl.ds(ORIGIN[0] + 32 * move, 32)
            values = block[32 * c : 32 * c + 32, :]
            if move < 2:
                edge = arrived(move + 1)[128 + c : 129 + c, :] * (0.5 * inside(move + 1))
                values = values - jnp.where(rows32 == ROWS - 1, edge, 0.0)
            if move > -2:
                edge = arrived(move - 1)[132 + c : 133 + c, :] * (0.5 * inside(move - 1))
                values = values + jnp.where(rows32 == 0, edge, 0.0)
            grid_b[0][c, rows, :] = jnp.where(deep[c, rows, :] > 0.5, values, 0.0)

    def operator(g, held, at):
        rows, after, before = pl.ds(at, 8), pl.ds(at + 1, 8), pl.ds(at - 1, 8)
        count = CLASSES[g]
        p = [held[c, rows, :] for c in range(count)]
        we = [grid_we[g][c, rows, :] for c in range(count)]
        ww = [grid_ww[g][rows, :]] + we[:-1]
        pe, pw = east_of(p, STEP[g]), west_of(p, STEP[g])
        residual = []
        for c in range(count):
            pull = (we[c] * pe[c] + ww[c] * pw[c]) + (
                grid_wn[g][c, rows, :] * held[c, after, :]
                + grid_wn[g][c, before, :] * held[c, before, :]
            )
            image = grid_dg[g][c, rows, :] * p[c] - pull
            residual.append(grid_b[g][c, rows, :] - image)
        return p, residual

    def span(g, low, high):
        return ORIGIN[g] + low, ORIGIN[g] + high

    def from_zero(g, low, high, held):
        def body(at):
            rows = pl.ds(at, 8)
            for c in range(CLASSES[g]):
                held[c, rows, :] = grid_b[g][c, rows, :] * grid_iv[g][c, rows, :]

        each_chunk(*span(g, low, high), body)

    def sweep(g, low, high, held, result):
        def body(at):
            rows = pl.ds(at, 8)
            p, residual = operator(g, held, at)
            for c in range(CLASSES[g]):
                result[c, rows, :] = p[c] + residual[c] * grid_iv[g][c, rows, :]

        each_chunk(*span(g, low, high), body)

    def restricted(g, low, high, held):
        def residual_rows(at):
            rows = pl.ds(at, 8)
            _, residual = operator(g, held, at)
            if g < 2:
                for c in range(CLASSES[g] // 2):
                    grid_r[g][c, rows, :] = residual[2 * c] + residual[2 * c + 1]
            else:
                even, east, west = pair_lanes(residual[0])
                grid_r[g][0, rows, :] = residual[0] + jnp.where(even, east, west)

        each_chunk(*span(g, low, high), residual_rows)

        def pair_rows(at):
            above = finer_rows(g + 1, at)
            for c in range(CLASSES[g + 1]):
                grid_b[g + 1][c, pl.ds(at, 8), :] = (
                    grid_r[g][c, pl.ds(above, 8, stride=2), :]
                    + grid_r[g][c, pl.ds(above + 1, 8, stride=2), :]
                )

        top = (high // 2 + 7) // 8 * 8
        each_chunk(*span(g + 1, low // 2 // 8 * 8, top), pair_rows)

    def corrected(g, low, high, held, correction):
        first, last = low // 2 // 8 * 8, (high // 2 + 7) // 8 * 8

        def body(at):
            above = finer_rows(g + 1, at)
            for c in range(CLASSES[g]):
                change = correction[c // 2, pl.ds(at, 8), :]
                for odd in (0, 1):
                    rows = pl.ds(above + odd, 8, stride=2)
                    held[c, rows, :] = held[c, rows, :] + change

        each_chunk(*span(g + 1, first, last), body)

    def coarse_source(reach):
        coarse_send[reach - 1] = grid_b[3][0, pl.ds(ORIGIN[3], 8), :]
        moves = LAT_MOVES[: 2 * reach]
        base = 0 if reach == 2 else 4
        copies = [
            send(coarse_send.at[reach - 1], coarse_got.at[base + i], 0, move)
            for i, move in enumerate(moves)
        ]
        launch(copies)
        for copy in copies:
            copy.wait_recv()
        upper = lax.broadcasted_iota(jnp.int32, (8, LANES), 0) >= 4

        def block(move):
            return coarse_got[base + moves.index(-move)] * inside(move)

        own = coarse_send[reach - 1]
        grid_b[3][0, pl.ds(ORIGIN[3], 8), :] = jnp.where(upper, pltpu.roll(block(1), 4, 0), own)
        lower = pltpu.roll(block(-1), 4, 0)
        if reach == 2:
            lower = jnp.where(upper, lower, block(-2))
            grid_b[3][0, pl.ds(ORIGIN[3] + 8, 8), :] = block(2)
        grid_b[3][0, pl.ds(ORIGIN[3] - 8, 8), :] = lower

    plans = (
        ((-64, 96), (-32, 48), (-16, 24), (-16, 24), (-16, 32), (-24, 56)),
        ((-24, 56), (-16, 32), (-8, 16), (-8, 16), (-8, 24), (-16, 48)),
        ((-16, 48), (-8, 24), (-8, 16), (-8, 16), (-8, 24), (-8, 40)),
    )
    for cycle in range(CYCLES):
        before0, down1, down2, up2, up1, after0 = plans[cycle]
        if cycle == 0:
            from_zero(0, *before0, grid_q[0])
        else:
            sweep(0, *before0, grid_p[0], grid_q[0])
        restricted(0, *before0, grid_q[0])
        from_zero(1, *down1, grid_q[1])
        restricted(1, *down1, grid_q[1])
        from_zero(2, *down2, grid_q[2])
        restricted(2, *down2, grid_q[2])
        if cycle > 0:
            coarse_source(3 - cycle)
        from_zero(3, -8, 16, grid_q[3])
        here, there_ = grid_q[3], grid_p[3]
        for _ in range(SWEEPS - 1):
            sweep(3, -8, 16, here, there_)
            here, there_ = there_, here
        corrected(2, *up2, grid_q[2], here)
        sweep(2, *up2, grid_q[2], grid_p[2])
        corrected(1, *up1, grid_q[1], grid_p[2])
        sweep(1, *up1, grid_q[1], grid_p[1])
        corrected(0, *after0, grid_q[0], grid_p[1])
        sweep(0, *after0, grid_q[0], grid_p[0])

    pressure = grid_p[0]
    own = pl.ds(ORIGIN[0], ROWS)
    p = [pressure[c, own, :] for c in range(4)]
    slope_east = [0.5 * (e - w) for e, w in zip(east_of(p, 1), west_of(p, 1))]
    slope_north = [
        0.5 * (pressure[c, pl.ds(ORIGIN[0] + 1, ROWS), :] - pressure[c, pl.ds(ORIGIN[0] - 1, ROWS), :])
        for c in range(4)
    ]
    stacked = jnp.concatenate(
        [jnp.concatenate(parts, axis=1) for parts in (p, slope_east, slope_north)], axis=0
    )
    ordered = exact_select(stacked, unchoice[...])
    p_out[...] = ordered[0:32]
    push_u = GRAVITY_STEP * ordered[32:64]
    push_v = GRAVITY_STEP * ordered[64:96]

    def finish(k, carry):
        rows = pl.ds(pl.multiple_of(k * ROWS, ROWS), ROWS)
        wet = k.astype(jnp.float32) < depth
        u_out[rows, :] = jnp.where(wet, u_star[rows, :] - push_u, 0.0)
        v_out[rows, :] = jnp.where(wet, v_star[rows, :] - push_v, 0.0)
        return carry

    lax.fori_loop(0, LEVELS, finish, 0)
    for copy in started:
        copy.wait_send()


def shards(lon_count, lat_count, u, v, t, depth, elevation):
    f32 = jnp.float32
    flat = (LEVELS * ROWS, COLS)
    block = pl.BlockSpec(memory_space=pltpu.VMEM)

    def grids(classes=CLASSES):
        return [pltpu.VMEM((c, h, LANES), f32) for c, h in zip(classes, HEIGHT)]

    outs = pl.pallas_call(
        functools.partial(kernel, lon_count, lat_count),
        out_shape=[jax.ShapeDtypeStruct(flat, f32)] * 3
        + [jax.ShapeDtypeStruct((ROWS, COLS), f32)],
        in_specs=[block] * 5,
        out_specs=[block] * 4,
        scratch_shapes=[
            pltpu.VMEM(flat, f32),
            pltpu.VMEM(flat, f32),
            pltpu.VMEM((2, 32, COLS), f32),
            pltpu.VMEM((2, 32, COLS), f32),
            pltpu.VMEM((2, 72, LANES), f32),
            pltpu.VMEM((2, 72, LANES), f32),
            pltpu.VMEM((2, 64, LANES), f32),
            pltpu.VMEM((2, 64, LANES), f32),
            pltpu.VMEM((128, LANES), f32),
            pltpu.VMEM((4, 128, LANES), f32),
            pltpu.VMEM((136, LANES), f32),
            pltpu.VMEM((4, 136, LANES), f32),
            pltpu.VMEM((2, 8, LANES), f32),
            pltpu.VMEM((6, 8, LANES), f32),
            pltpu.VMEM((WIDE, WIDE), jnp.bfloat16),
            pltpu.VMEM((WIDE, COLS), jnp.bfloat16),
            pltpu.VMEM((4, HEIGHT[0], LANES), f32),
            grids(),
            grids(),
            grids(),
            grids(),
            [pltpu.VMEM((h, LANES), f32) for h in HEIGHT],
            grids(),
            grids(),
            grids(),
            grids(),
            pltpu.SemaphoreType.DMA((24,)),
            pltpu.SemaphoreType.DMA((24,)),
        ],
        compiler_params=pltpu.CompilerParams(
            collective_id=0, has_side_effects=True, vmem_limit_bytes=32 << 20
        ),
    )(u.reshape(flat), v.reshape(flat), t.reshape(flat), depth, elevation)
    shape = (LEVELS, ROWS, COLS)
    return outs[0].reshape(shape), outs[1].reshape(shape), outs[2].reshape(shape), outs[3]


def solution(mesh):
    spec3, spec2 = P(None, "lat", "lon"), P("lat", "lon")
    return jax.shard_map(
        functools.partial(shards, mesh.shape["lon"], mesh.shape["lat"]),
        mesh=mesh,
        in_specs=(spec3, spec3, spec3, spec2, spec2),
        out_specs=(spec3, spec3, spec3, spec2),
        check_vma=False,
    )
```

time: 833 us -> 65 us (0.08)
  starting transfers between devices: 407 us -> 0 us
  waiting for transfers between devices: 393 us -> 0 us
  Pallas kernels: 0 us -> 56.9 us
  other arithmetic: 13.9 us -> 0 us
    ppermute x128 -> x0, starting transfers between devices: 407 us -> none  [the longest x64 269 us: with_halo(): lax.ppermute(lax.slice_in_dim(block, 0, width, axis=dim), axis, backward)]
    ppermute x128 -> x0, waiting for transfers between devices: 393 us -> none  [the longest x64 376 us: with_halo(): lax.ppermute(lax.slice_in_dim(block, block.shape[dim] - width, None, axis...]
    pallas_call x0 -> x1, Pallas kernels: none -> 56.9 us  [shards(): pl.pallas_call(functools.partial(kernel, lon_count, lat_count), out_shape...]
    slice x106 -> x0, local copies, waits for them, and re-layouts: 11.3 us -> none  [the longest x18 3.58 us: restrict(): return paired[..., 0::2] + paired[..., 1::2]]
  transfers between devices with their start and end apart: 128 -> 0, of which waited for: 65 -> 0; matrix products, arithmetic and copies ran while one was open for 0% -> 0% of each run, Pallas kernels for 0% -> 0%
where the time goes in v1:
time: 65 us; the launch traced here: 64.7 us
  Pallas kernels  56.9 us (88%)
  local copies, waits for them, and re-layouts  7.08 us (11%)
  between operations  0.65 us (1%)
    pallas_call x1, Pallas kernels, shards(): pl.pallas_call(functools.partial(kernel, lon_count, lat_count), out_shape...  56.9 us
    unnamed x14, local copies, waits for them, and re-layouts  7.08 us

profile of v1, /device:TPU:32, one launch (start us, length us, event | category | flops | bytes accessed | tf_op | source)
XLA Modules:
  0.0 64.7 jit_solution(12976102070837039524)
XLA Ops:
  0.6 0.0 copy-start
  0.6 0.9 %copy-done = f32[8,32,256]{2,1,0:T(8,128)S(1)} copy-done((f32[8,32,256]{2,1,0:T(8,128)S(1)}, f32[8,32,256]{2,1,0:T(8,128)}, u32[]{:S(2)}) %copy-start) | copy-done | bytes 262168
  1.6 0.0 copy-start.1
  1.6 0.9 %copy-done.1 = f32[8,32,256]{2,1,0:T(8,128)S(1)} copy-done((f32[8,32,256]{2,1,0:T(8,128)S(1)}, f32[8,32,256]{2,1,0:T(8,128)}, u32[]{:S(2)}) %copy-start.1) | copy-done | bytes 262168
  2.5 0.0 copy-start.2
  2.5 0.9 %copy-done.2 = f32[8,32,256]{2,1,0:T(8,128)S(1)} copy-done((f32[8,32,256]{2,1,0:T(8,128)S(1)}, f32[8,32,256]{2,1,0:T(8,128)}, u32[]{:S(2)}) %copy-start.2) | copy-done | bytes 262168
  3.5 0.0 copy-start.3
  3.5 0.8 %copy-done.3 = s32[32,256]{1,0:T(8,128)S(1)} copy-done((s32[32,256]{1,0:T(8,128)S(1)}, s32[32,256]{1,0:T(8,128)}, u32[]{:S(2)}) %copy-start.3) | copy-done | bytes 32792
  4.2 0.0 copy-start.4
  4.2 0.8 %copy-done.4 = f32[32,256]{1,0:T(8,128)S(1)} copy-done((f32[32,256]{1,0:T(8,128)S(1)}, f32[32,256]{1,0:T(8,128)}, u32[]{:S(2)}) %copy-start.4) | copy-done | bytes 32792
  5.0 56.9 %shard_map.84 = (f32[256,256]{1,0:T(8,128)S(1)}, f32[256,256]{1,0:T(8,128)S(1)}, f32[256,256]{1,0:T(8,128)S(1)}, f32[32,256]{1,0:T(8,128)S(1)}) custom-call(f32[256,256]{1,0:T(8,128)S(1)} %bitcast.6, f32[256,256]{1,0:T(8,128)S(1)} %bitcast.7, f32[256,256]{1,0:T(8,128)S(1)} %bitcast.8, s32[32,256]{1,0:T(8,128)S(1)} %copy-done.3, f32[32,256]{1,0:T(8,128)S(1)} %copy-done.4), custom_call_target="tpu_custom_call" | custom-call | tf_op jit(solution)/shard_map/pallas_call | solution.py:604
  62.0 0.7 %copy.13 = f32[8,32,256]{2,1,0:T(8,128)} copy(f32[8,32,256]{2,1,0:T(8,128)S(1)} %bitcast.11) | data formatting | bytes 524288
  62.7 0.7 %copy.14 = f32[8,32,256]{2,1,0:T(8,128)} copy(f32[8,32,256]{2,1,0:T(8,128)S(1)} %bitcast.10) | data formatting | bytes 524288
  63.4 0.7 %copy.15 = f32[8,32,256]{2,1,0:T(8,128)} copy(f32[8,32,256]{2,1,0:T(8,128)S(1)} %bitcast.9) | data formatting | bytes 524288
  64.1 0.6 copy.16
Async XLA Ops:
  0.6 1.0 %copy-start = (f32[8,32,256]{2,1,0:T(8,128)S(1)}, f32[8,32,256]{2,1,0:T(8,128)}, u32[]{:S(2)}) copy-start(f32[8,32,256]{2,1,0:T(8,128)} %param.5) | copy-start | bytes 786436
  1.6 0.9 %copy-start.1 = (f32[8,32,256]{2,1,0:T(8,128)S(1)}, f32[8,32,256]{2,1,0:T(8,128)}, u32[]{:S(2)}) copy-start(f32[8,32,256]{2,1,0:T(8,128)} %param.6) | copy-start | bytes 786436
  2.5 0.9 %copy-start.2 = (f32[8,32,256]{2,1,0:T(8,128)S(1)}, f32[8,32,256]{2,1,0:T(8,128)}, u32[]{:S(2)}) copy-start(f32[8,32,256]{2,1,0:T(8,128)} %param.7) | copy-start | bytes 786436
  3.5 0.8 %copy-start.3 = (s32[32,256]{1,0:T(8,128)S(1)}, s32[32,256]{1,0:T(8,128)}, u32[]{:S(2)}) copy-start(s32[32,256]{1,0:T(8,128)} %depth_ref.1) | copy-start | bytes 98308
  4.2 0.8 %copy-start.4 = (f32[32,256]{1,0:T(8,128)S(1)}, f32[32,256]{1,0:T(8,128)}, u32[]{:S(2)}) copy-start(f32[32,256]{1,0:T(8,128)} %elevation_ref.1) | copy-start | bytes 98308

commit v2 on v1

--- a/solution.py
+++ b/solution.py
@@ -25,8 +25,8 @@
 
 CLASSES = (4, 2, 1, 1)
 STEP = (1, 1, 1, 2)
-ORIGIN = (72, 40, 24, 16)
-HEIGHT = (176, 96, 56, 40)
+ORIGIN = (48, 32, 24, 16)
+HEIGHT = (128, 80, 56, 40)
 MASS = tuple(MASS_TERM * 4.0**g for g in range(4))
 
 LAT_MOVES = (1, -1, 2, -2)
@@ -76,17 +76,25 @@
 def kernel(
     lon_count,
     lat_count,
+    u_far,
+    v_far,
+    t_far,
+    depth_far,
+    elevation_far,
+    u_home,
+    v_home,
+    t_home,
+    p_out,
+    push_u_out,
+    push_v_out,
     u_ref,
     v_ref,
     t_ref,
     depth_ref,
     elevation_ref,
-    u_out,
-    v_out,
-    t_out,
-    p_out,
     u_star,
     v_star,
+    t_out,
     rows_send,
     rows_got,
     cols_send,
@@ -95,8 +103,14 @@
     mean_got,
     deep_send,
     deep_got,
+    deep_got_far,
     source_send,
     source_got,
+    source_got_far,
+    ends_send,
+    ends_got,
+    weight_send,
+    weight_got,
     coarse_send,
     coarse_got,
     choice,
@@ -111,6 +125,7 @@
     grid_dg,
     grid_iv,
     grid_r,
+    load_sem,
     send_sem,
     recv_sem,
 ):
@@ -152,6 +167,23 @@
             barrier, inc=1, device_id=there(lon_move, lat_move), device_id_type=MESH_IDS
         )
 
+    loads = [
+        pltpu.make_async_copy(far, near, load_sem.at[i])
+        for i, (far, near) in enumerate(
+            (
+                (depth_far, depth_ref),
+                (elevation_far, elevation_ref),
+                (u_far, u_ref),
+                (v_far, v_ref),
+                (t_far, t_ref),
+            )
+        )
+    ]
+    for load in loads:
+        load.start()
+    for load in loads:
+        load.wait()
+
     depth = depth_ref[...].astype(jnp.float32)
     lane8 = lax.broadcasted_iota(jnp.int32, (8, LANES), 1)
     fields = (u_ref, v_ref, t_ref)
@@ -175,6 +207,7 @@
     zero8 = jnp.zeros((8, LANES), jnp.float32)
     at_last, at_first = lax.fori_loop(0, 32, pack, (zero8, zero8), unroll=4)
     elevation = elevation_ref[...]
+    deep_send[0] = depth
     for side, edge, tile in ((0, at_last, 1), (1, at_first, 0)):
         cut = slice(tile * LANES, (tile + 1) * LANES)
         cols_send[side, 0:32, :] = depth[:, cut]
@@ -190,6 +223,18 @@
     ]
     launch(first)
 
+    def depth_sends(part):
+        source = deep_send.at[part]
+        return [
+            send(source, deep_got.at[part, 0], 0, 1),
+            send(source, deep_got.at[part, 1], 0, -1),
+            send(source.at[pl.ds(ROWS - 8, 8)], deep_got_far.at[part, 0], 0, 2),
+            send(source.at[pl.ds(0, 8)], deep_got_far.at[part, 1], 0, -2),
+        ]
+
+    depth_copies = depth_sends(0)
+    launch(depth_copies)
+
     def order(n):
         return ((((n & 127) + 32) & 127) << 2) + (n >> 7)
 
@@ -217,16 +262,11 @@
         copy.wait_recv()
 
     west_tile, east_tile = cols_got.at[0], cols_got.at[1]
-    depth_wide = jnp.concatenate([west_tile[0:32, :], depth, east_tile[0:32, :]], axis=1)
-    by_class = jnp.dot(
-        depth_wide.astype(jnp.bfloat16), choice[...], preferred_element_type=jnp.float32
-    )
-    for c in range(4):
-        deep_send[32 * c : 32 * c + 32, :] = by_class[:, LANES * c : LANES * (c + 1)]
-    depth_copies = [
-        send(deep_send, deep_got.at[i], 0, move) for i, move in enumerate(LAT_MOVES)
-    ]
-    launch(depth_copies)
+    deep_send[1, :, 0:LANES] = west_tile[0:32, :]
+    deep_send[1, :, LANES:COLS] = east_tile[0:32, :]
+    more_depth = depth_sends(1)
+    launch(more_depth)
+    depth_copies = depth_copies + more_depth
 
     row = lax.broadcasted_iota(jnp.int32, (ROWS, COLS), 0)
     column = lax.broadcasted_iota(jnp.int32, (ROWS, COLS), 1)
@@ -317,6 +357,14 @@
         return carry
 
     lax.fori_loop(0, LEVELS, tracer, 0)
+    stores = [
+        pltpu.make_async_copy(near, far, load_sem.at[i])
+        for i, (near, far) in enumerate(
+            ((u_star, u_home), (v_star, v_home), (t_out, t_home))
+        )
+    ]
+    for store in stores:
+        store.start()
 
     for copy in mean_copies:
         copy.wait_recv()
@@ -328,6 +376,7 @@
     north_v = jnp.where(wide_row == ROWS - 1, 0.0, pltpu.roll(wide_v, ROWS - 1, 0))
     south_v = jnp.where(wide_row == 0, 0.0, pltpu.roll(wide_v, 1, 0))
     across = pltpu.roll(wide_u, WIDE - 1, 1) - pltpu.roll(wide_u, 1, 1)
+    depth_wide = jnp.concatenate([west_tile[0:32, :], depth, east_tile[0:32, :]], axis=1)
     source = jnp.where(
         depth_wide > 0.5, wide_eta - 0.5 * (across + (north_v - south_v)), 0.0
     )
@@ -337,11 +386,16 @@
     by_class = exact_select(jnp.concatenate([source, ends], axis=0), choice[...])
     for c in range(4):
         cut = slice(LANES * c, LANES * (c + 1))
-        source_send[32 * c : 32 * c + 32, :] = by_class[0:32, cut]
-        source_send[128 + c : 129 + c, :] = by_class[32:33, cut]
-        source_send[132 + c : 133 + c, :] = by_class[33:34, cut]
+        source_send[c] = by_class[0:32, cut]
+        ends_send[c : c + 1, :] = by_class[32:33, cut]
+        ends_send[4 + c : 5 + c, :] = by_class[33:34, cut]
     source_copies = [
-        send(source_send, source_got.at[i], 0, move) for i, move in enumerate(LAT_MOVES)
+        send(ends_send, ends_got.at[i], 0, move) for i, move in enumerate(LAT_MOVES)
+    ] + [
+        send(source_send, source_got.at[0], 0, 1),
+        send(source_send, source_got.at[1], 0, -1),
+        send(source_send.at[:, pl.ds(ROWS - 8, 8)], source_got_far.at[0], 0, 2),
+        send(source_send.at[:, pl.ds(0, 8)], source_got_far.at[1], 0, -2),
     ]
     launch(source_copies)
 
@@ -351,15 +405,23 @@
     def slot_of(lat_move):
         return LAT_MOVES.index(-lat_move)
 
-    for move in range(-2, 3):
-        for c in range(4):
-            rows = pl.ds(ORIGIN[0] + 32 * move, 32)
-            if move == 0:
-                deep[c, rows, :] = deep_send[32 * c : 32 * c + 32, :]
-            else:
-                deep[c, rows, :] = (
-                    deep_got[slot_of(move), 32 * c : 32 * c + 32, :] * inside(move)
-                )
+    def wide_depth(own, halo, mask):
+        return mask * jnp.concatenate([halo[:, 0:LANES], own, halo[:, LANES:COLS]], axis=1)
+
+    blocks = [
+        wide_depth(deep_got_far[0, 0], deep_got_far[1, 0], inside(-2)),
+        wide_depth(deep_got[0, 0], deep_got[1, 0], inside(-1)),
+        wide_depth(deep_send[0], deep_send[1], 1.0),
+        wide_depth(deep_got[0, 1], deep_got[1, 1], inside(1)),
+        wide_depth(deep_got_far[0, 1], deep_got_far[1, 1], inside(2)),
+    ]
+    by_class = jnp.dot(
+        jnp.concatenate(blocks, axis=0).astype(jnp.bfloat16),
+        choice[...],
+        preferred_element_type=jnp.float32,
+    )
+    for c in range(4):
+        deep[c, pl.ds(ORIGIN[0] - 40, 112), :] = by_class[:, LANES * c : LANES * (c + 1)]
 
     def finish_weights(g, rows):
         we = [grid_we[g][c, rows, :] for c in range(CLASSES[g])]
@@ -380,7 +442,7 @@
             grid_wn[0][c, rows, :] = jnp.minimum(columns[c], north)
 
     def whole(g):
-        return ORIGIN[g] - (64 >> g), ORIGIN[g] + ((96 >> g) + 7) // 8 * 8
+        return tuple(ORIGIN[g] + end for end in ((-40, 72), (-24, 40), (-16, 24), (0, 8))[g])
 
     def pair_lanes(values):
         even = (lax.broadcasted_iota(jnp.int32, values.shape, 1) & 1) == 0
@@ -415,27 +477,53 @@
                 grid_wn[g][0, rows, :] = wn + jnp.where(even, east, west)
 
         each_chunk(*whole(g), coarse_weights)
-        each_chunk(*whole(g), lambda at, g=g: finish_weights(g, pl.ds(at, 8)))
+        if g < 3:
+            each_chunk(*whole(g), lambda at, g=g: finish_weights(g, pl.ds(at, 8)))
+
+    upper = lax.broadcasted_iota(jnp.int32, (8, LANES), 0) >= 4
+
+    def around(held, own, got, moves):
+        def block(move):
+            return got[moves.index(-move)][...] * inside(move)
+
+        held[0, pl.ds(ORIGIN[3], 8), :] = jnp.where(upper, pltpu.roll(block(1), 4, 0), own)
+        lower = pltpu.roll(block(-1), 4, 0)
+        if len(moves) == 4:
+            lower = jnp.where(upper, lower, block(-2))
+            held[0, pl.ds(ORIGIN[3] + 8, 8), :] = block(2)
+        held[0, pl.ds(ORIGIN[3] - 8, 8), :] = lower
+
+    weight_send[0:8, :] = grid_we[3][0, pl.ds(ORIGIN[3], 8), :]
+    weight_send[8:16, :] = grid_wn[3][0, pl.ds(ORIGIN[3], 8), :]
+    weight_copies = [
+        send(weight_send, weight_got.at[i], 0, move) for i, move in enumerate(LAT_MOVES)
+    ]
+    launch(weight_copies)
 
     for copy in source_copies:
         copy.wait_recv()
 
-    def arrived(move):
-        return source_send if move == 0 else source_got.at[slot_of(move)]
-
     rows32 = lax.broadcasted_iota(jnp.int32, (ROWS, LANES), 0)
-    for move in range(-2, 3):
-        block = arrived(move)
-        for c in range(4):
-            rows = pl.ds(ORIGIN[0] + 32 * move, 32)
-            values = block[32 * c : 32 * c + 32, :]
-            if move < 2:
-                edge = arrived(move + 1)[128 + c : 129 + c, :] * (0.5 * inside(move + 1))
-                values = values - jnp.where(rows32 == ROWS - 1, edge, 0.0)
-            if move > -2:
-                edge = arrived(move - 1)[132 + c : 133 + c, :] * (0.5 * inside(move - 1))
-                values = values + jnp.where(rows32 == 0, edge, 0.0)
-            grid_b[0][c, rows, :] = jnp.where(deep[c, rows, :] > 0.5, values, 0.0)
+
+    def ends(move, spot):
+        held = ends_send if move == 0 else ends_got.at[slot_of(move)]
+        return held[spot : spot + 1, :] * (0.5 * inside(move))
+
+    def place_source(c, move, first, values):
+        rows = pl.ds(ORIGIN[0] + first, values.shape[0])
+        at = rows32[: values.shape[0]] + (first - 32 * move)
+        if move < 2:
+            values = values - jnp.where(at == ROWS - 1, ends(move + 1, c), 0.0)
+        if move > -2:
+            values = values + jnp.where(at == 0, ends(move - 1, 4 + c), 0.0)
+        grid_b[0][c, rows, :] = jnp.where(deep[c, rows, :] > 0.5, values, 0.0)
+
+    for c in range(4):
+        place_source(c, -2, -40, source_got_far[0, c])
+        place_source(c, -1, -32, source_got[0, c])
+        place_source(c, 0, 0, source_send[c])
+        place_source(c, 1, 32, source_got[1, c])
+        place_source(c, 2, 64, source_got_far[1, c])
 
     def operator(g, held, at):
         rows, after, before = pl.ds(at, 8), pl.ds(at + 1, 8), pl.ds(at - 1, 8)
@@ -511,32 +599,27 @@
 
         each_chunk(*span(g + 1, first, last), body)
 
-    def coarse_source(reach):
-        coarse_send[reach - 1] = grid_b[3][0, pl.ds(ORIGIN[3], 8), :]
+    def coarse_source(cycle, reach):
+        coarse_send[cycle] = grid_b[3][0, pl.ds(ORIGIN[3], 8), :]
         moves = LAT_MOVES[: 2 * reach]
-        base = 0 if reach == 2 else 4
+        got = coarse_got.at[pl.ds(4 * cycle, 2 * reach)]
         copies = [
-            send(coarse_send.at[reach - 1], coarse_got.at[base + i], 0, move)
-            for i, move in enumerate(moves)
+            send(coarse_send.at[cycle], got.at[i], 0, move) for i, move in enumerate(moves)
         ]
         launch(copies)
+        if cycle == 0:
+            for copy in weight_copies:
+                copy.wait_recv()
+            for held, first in ((grid_we[3], 0), (grid_wn[3], 8)):
+                cut = pl.ds(first, 8)
+                around(held, weight_send[cut, :], [weight_got.at[i, cut] for i in range(4)], LAT_MOVES)
+            each_chunk(ORIGIN[3] - 8, ORIGIN[3] + 16, lambda at: finish_weights(3, pl.ds(at, 8)))
         for copy in copies:
             copy.wait_recv()
-        upper = lax.broadcasted_iota(jnp.int32, (8, LANES), 0) >= 4
-
-        def block(move):
-            return coarse_got[base + moves.index(-move)] * inside(move)
-
-        own = coarse_send[reach - 1]
-        grid_b[3][0, pl.ds(ORIGIN[3], 8), :] = jnp.where(upper, pltpu.roll(block(1), 4, 0), own)
-        lower = pltpu.roll(block(-1), 4, 0)
-        if reach == 2:
-            lower = jnp.where(upper, lower, block(-2))
-            grid_b[3][0, pl.ds(ORIGIN[3] + 8, 8), :] = block(2)
-        grid_b[3][0, pl.ds(ORIGIN[3] - 8, 8), :] = lower
+        around(grid_b[3], coarse_send[cycle], [got.at[i] for i in range(2 * reach)], moves)
 
     plans = (
-        ((-64, 96), (-32, 48), (-16, 24), (-16, 24), (-16, 32), (-24, 56)),
+        ((-40, 72), (-24, 40), (-16, 24), (-8, 16), (-16, 32), (-24, 56)),
         ((-24, 56), (-16, 32), (-8, 16), (-8, 16), (-8, 24), (-16, 48)),
         ((-16, 48), (-8, 24), (-8, 16), (-8, 16), (-8, 24), (-8, 40)),
     )
@@ -550,9 +633,8 @@
         from_zero(1, *down1, grid_q[1])
         restricted(1, *down1, grid_q[1])
         from_zero(2, *down2, grid_q[2])
-        restricted(2, *down2, grid_q[2])
-        if cycle > 0:
-            coarse_source(3 - cycle)
+        restricted(2, -8, 16, grid_q[2])
+        coarse_source(cycle, 1 if cycle == 2 else 2)
         from_zero(3, -8, 16, grid_q[3])
         here, there_ = grid_q[3], grid_p[3]
         for _ in range(SWEEPS - 1):
@@ -578,19 +660,23 @@
     )
     ordered = exact_select(stacked, unchoice[...])
     p_out[...] = ordered[0:32]
-    push_u = GRAVITY_STEP * ordered[32:64]
-    push_v = GRAVITY_STEP * ordered[64:96]
-
-    def finish(k, carry):
-        rows = pl.ds(pl.multiple_of(k * ROWS, ROWS), ROWS)
-        wet = k.astype(jnp.float32) < depth
-        u_out[rows, :] = jnp.where(wet, u_star[rows, :] - push_u, 0.0)
-        v_out[rows, :] = jnp.where(wet, v_star[rows, :] - push_v, 0.0)
-        return carry
-
-    lax.fori_loop(0, LEVELS, finish, 0)
+    push_u_out[...] = GRAVITY_STEP * ordered[32:64]
+    push_v_out[...] = GRAVITY_STEP * ordered[64:96]
+    for store in stores:
+        store.wait()
     for copy in started:
         copy.wait_send()
+
+
+def finish(u_star, v_star, t, p, push_u, push_v, depth_ref, u_out, v_out, t_out, p_out):
+    depth = depth_ref[...]
+    p_out[...] = p[...]
+    t_out[...] = t[...]
+    for k in range(LEVELS):
+        rows = slice(k * ROWS, (k + 1) * ROWS)
+        wet = depth > k
+        u_out[rows, :] = jnp.where(wet, u_star[rows, :] - push_u[...], 0.0)
+        v_out[rows, :] = jnp.where(wet, v_star[rows, :] - push_v[...], 0.0)
 
 
 def shards(lon_count, lat_count, u, v, t, depth, elevation):
@@ -601,13 +687,20 @@
     def grids(classes=CLASSES):
         return [pltpu.VMEM((c, h, LANES), f32) for c, h in zip(classes, HEIGHT)]
 
-    outs = pl.pallas_call(
+    anywhere = pl.BlockSpec(memory_space=pl.ANY)
+    held = pl.pallas_call(
         functools.partial(kernel, lon_count, lat_count),
         out_shape=[jax.ShapeDtypeStruct(flat, f32)] * 3
-        + [jax.ShapeDtypeStruct((ROWS, COLS), f32)],
-        in_specs=[block] * 5,
-        out_specs=[block] * 4,
+        + [jax.ShapeDtypeStruct((ROWS, COLS), f32)] * 3,
+        in_specs=[anywhere] * 5,
+        out_specs=[anywhere] * 3 + [block] * 3,
         scratch_shapes=[
+            pltpu.VMEM(flat, f32),
+            pltpu.VMEM(flat, f32),
+            pltpu.VMEM(flat, f32),
+            pltpu.VMEM((ROWS, COLS), jnp.int32),
+            pltpu.VMEM((ROWS, COLS), f32),
+            pltpu.VMEM(flat, f32),
             pltpu.VMEM(flat, f32),
             pltpu.VMEM(flat, f32),
             pltpu.VMEM((2, 32, COLS), f32),
@@ -616,12 +709,18 @@
             pltpu.VMEM((2, 72, LANES), f32),
             pltpu.VMEM((2, 64, LANES), f32),
             pltpu.VMEM((2, 64, LANES), f32),
-            pltpu.VMEM((128, LANES), f32),
-            pltpu.VMEM((4, 128, LANES), f32),
-            pltpu.VMEM((136, LANES), f32),
-            pltpu.VMEM((4, 136, LANES), f32),
-            pltpu.VMEM((2, 8, LANES), f32),
-            pltpu.VMEM((6, 8, LANES), f32),
+            pltpu.VMEM((2, ROWS, COLS), f32),
+            pltpu.VMEM((2, 2, ROWS, COLS), f32),
+            pltpu.VMEM((2, 2, 8, COLS), f32),
+            pltpu.VMEM((4, ROWS, LANES), f32),
+            pltpu.VMEM((2, 4, ROWS, LANES), f32),
+            pltpu.VMEM((2, 4, 8, LANES), f32),
+            pltpu.VMEM((8, LANES), f32),
+            pltpu.VMEM((4, 8, LANES), f32),
+            pltpu.VMEM((16, LANES), f32),
+            pltpu.VMEM((4, 16, LANES), f32),
+            pltpu.VMEM((CYCLES, 8, LANES), f32),
+            pltpu.VMEM((10, 8, LANES), f32),
             pltpu.VMEM((WIDE, WIDE), jnp.bfloat16),
             pltpu.VMEM((WIDE, COLS), jnp.bfloat16),
             pltpu.VMEM((4, HEIGHT[0], LANES), f32),
@@ -634,13 +733,22 @@
             grids(),
             grids(),
             grids(),
-            pltpu.SemaphoreType.DMA((24,)),
-            pltpu.SemaphoreType.DMA((24,)),
+            pltpu.SemaphoreType.DMA((5,)),
+            pltpu.SemaphoreType.DMA((40,)),
+            pltpu.SemaphoreType.DMA((40,)),
         ],
         compiler_params=pltpu.CompilerParams(
-            collective_id=0, has_side_effects=True, vmem_limit_bytes=32 << 20
+            collective_id=0, has_side_effects=True, vmem_limit_bytes=60 << 20
         ),
     )(u.reshape(flat), v.reshape(flat), t.reshape(flat), depth, elevation)
+    outs = pl.pallas_call(
+        finish,
+        out_shape=[jax.ShapeDtypeStruct(flat, f32)] * 3
+        + [jax.ShapeDtypeStruct((ROWS, COLS), f32)],
+        in_specs=[block] * 7,
+        out_specs=[block] * 4,
+        compiler_params=pltpu.CompilerParams(vmem_limit_bytes=60 << 20),
+    )(*held, depth)
     shape = (LEVELS, ROWS, COLS)
     return outs[0].reshape(shape), outs[1].reshape(shape), outs[2].reshape(shape), outs[3]
 

time: 65 us -> 53.9 us (0.83)
  the two profiles are of different devices: /device:TPU:32 before, /device:TPU:2 now
where the time goes in v2:
time: 53.9 us; the launch traced here: 53.8 us
  Pallas kernels  53.1 us (99%)
  between operations  0.64 us (1%)
    pallas_call x1, Pallas kernels, shards(): pl.pallas_call(functools.partial(kernel, lon_count, lat_count), out_shape...  51 us
    pallas_call x1, Pallas kernels, shards(): pl.pallas_call(finish, out_shape=[jax.ShapeDtypeStruct(flat, f32)] * 3 +...  2.08 us

profile of v2, /device:TPU:2, one launch (start us, length us, event | category | flops | bytes accessed | tf_op | source)
XLA Modules:
  0.0 53.8 jit_solution(3513804358576344908)
XLA Ops:
  0.6 51.0 %shard_map.84 = (f32[256,256]{1,0:T(8,128)}, f32[256,256]{1,0:T(8,128)}, f32[256,256]{1,0:T(8,128)}, f32[32,256]{1,0:T(8,128)}, f32[32,256]{1,0:T(8,128)}, /*index=5*/f32[32,256]{1,0:T(8,128)}) custom-call(f32[256,256]{1,0:T(8,128)} %bitcast.6, f32[256,256]{1,0:T(8,128)} %bitcast.7, f32[256,256]{1,0:T(8,128)} %bitcast.8, s32[32,256]{1,0:T(8,128)} %depth_ref.1, ...), custom_call_target="tpu_custom_call" | custom-call | tf_op jit(solution)/shard_map/pallas_call | solution.py:691
  51.7 2.1 %shard_map.85 = (f32[256,256]{1,0:T(8,128)}, f32[256,256]{1,0:T(8,128)}, f32[256,256]{1,0:T(8,128)}, f32[32,256]{1,0:T(8,128)}) custom-call(f32[256,256]{1,0:T(8,128)} %get-tuple-element.14.u_star, f32[256,256]{1,0:T(8,128)} %get-tuple-element.15.v_star, f32[256,256]{1,0:T(8,128)} %get-tuple-element.16.t, f32[32,256]{1,0:T(8,128)} %get-tuple-element.17.p, ...), custom_call_target="tpu_custom_call" | custom-call | tf_op jit(solution)/shard_map/pallas_call | solution.py:744

commit v3 on v2

--- a/solution.py
+++ b/solution.py
@@ -30,6 +30,7 @@
 MASS = tuple(MASS_TERM * 4.0**g for g in range(4))
 
 LAT_MOVES = (1, -1, 2, -2)
+EARLY_LEVELS = 3
 
 
 def east_of(parts, step):
@@ -215,13 +216,15 @@
         cols_send[side, 64:72, :] = edge
 
     pl.semaphore_wait(barrier, 2 + len(LAT_MOVES))
-    first = [
-        send(cols_send.at[0], cols_got.at[0], 1, 0),
-        send(cols_send.at[1], cols_got.at[1], -1, 0),
+    row_copies = [
         send(rows_send.at[0], rows_got.at[0], 0, 1),
         send(rows_send.at[1], rows_got.at[1], 0, -1),
     ]
-    launch(first)
+    column_copies = [
+        send(cols_send.at[0], cols_got.at[0], 1, 0),
+        send(cols_send.at[1], cols_got.at[1], -1, 0),
+    ]
+    launch(column_copies + row_copies)
 
     def depth_sends(part):
         source = deep_send.at[part]
@@ -235,6 +238,82 @@
     depth_copies = depth_sends(0)
     launch(depth_copies)
 
+    row_number = lax.broadcasted_iota(jnp.int32, (ROWS, LANES), 0)
+    place = (lat * ROWS + row_number).astype(jnp.float32)
+    angle = jnp.pi * ((place + 0.5) / (ROWS * lat_count) - 0.5)
+    turning = CORIOLIS * jnp.sin(angle)
+    rotation = jnp.concatenate([turning, turning], axis=1)
+
+    row = lax.broadcasted_iota(jnp.int32, (ROWS, COLS), 0)
+    column = lax.broadcasted_iota(jnp.int32, (ROWS, COLS), 1)
+    on_east, on_west = column == COLS - 1, column == 0
+    on_north, on_south = row == ROWS - 1, row == 0
+
+    def beside(values, east_edge, west_edge, north_edge, south_edge):
+        return (
+            jnp.where(on_east, east_edge, pltpu.roll(values, COLS - 1, 1)),
+            jnp.where(on_west, west_edge, pltpu.roll(values, 1, 1)),
+            jnp.where(on_north, north_edge, pltpu.roll(values, ROWS - 1, 0)),
+            jnp.where(on_south, south_edge, pltpu.roll(values, 1, 0)),
+        )
+
+    def laplace(faces, values, nearby):
+        terms = [jnp.where(face, near - values, 0.0) for face, near in zip(faces, nearby)]
+        return (terms[0] + terms[1]) + (terms[2] + terms[3])
+
+    def momentum(faces, u, near_u, v, near_v):
+        guess_u = u + TIME_STEP * (VISCOSITY * laplace(faces, u, near_u) + rotation * v)
+        guess_v = v + TIME_STEP * (VISCOSITY * laplace(faces, v, near_v) - rotation * u)
+        return guess_u, guess_v
+
+    inner_depth = [jnp.minimum(depth, near) for near in beside(depth, 0.0, 0.0, 0.0, 0.0)]
+
+    def inner(k, carry):
+        sum_u, sum_v = carry
+        level = k.astype(jnp.float32)
+        faces = [level < limit for limit in inner_depth]
+        rows = pl.ds(pl.multiple_of(k * ROWS, ROWS), ROWS)
+        u, v = u_ref[rows, :], v_ref[rows, :]
+        near_u, near_v = beside(u, 0.0, 0.0, 0.0, 0.0), beside(v, 0.0, 0.0, 0.0, 0.0)
+        guess_u, guess_v = momentum(faces, u, near_u, v, near_v)
+        wet = level < depth
+        return sum_u + jnp.where(wet, guess_u, 0.0), sum_v + jnp.where(wet, guess_v, 0.0)
+
+    zero = jnp.zeros((ROWS, COLS), jnp.float32)
+    sum_u, sum_v = lax.fori_loop(0, LEVELS, inner, (zero, zero))
+    gain = TIME_STEP * VISCOSITY / LEVELS
+
+    for copy in row_copies:
+        copy.wait_recv()
+    north_depth = rows_got[1, 24:25, :] * inside(1)
+    south_depth = rows_got[0, 24:25, :] * inside(-1)
+    level8 = lax.broadcasted_iota(jnp.int32, (LEVELS, COLS), 0).astype(jnp.float32)
+
+    def row_flux(f, side, limit):
+        step = rows_got[side, 8 * f : 8 * f + 8, :] - rows_send[1 - side, 8 * f : 8 * f + 8, :]
+        return gain * jnp.sum(jnp.where(level8 < limit, step, 0.0), axis=0, keepdims=True)
+
+    north_limit = jnp.minimum(depth[ROWS - 1 : ROWS, :], north_depth)
+    south_limit = jnp.minimum(depth[0:1, :], south_depth)
+
+    def mean(f, total):
+        return (
+            total * (1.0 / LEVELS)
+            + jnp.where(on_north, row_flux(f, 1, north_limit), 0.0)
+            + jnp.where(on_south, row_flux(f, 0, south_limit), 0.0)
+        )
+
+    mean_u, mean_v = mean(0, sum_u), mean(1, sum_v)
+    for side, tile in ((0, 1), (1, 0)):
+        cut = slice(tile * LANES, (tile + 1) * LANES)
+        mean_send[side, 0:32, :] = mean_u[:, cut]
+        mean_send[side, 32:64, :] = mean_v[:, cut]
+    mean_copies = [
+        send(mean_send.at[0], mean_got.at[0], 1, 0),
+        send(mean_send.at[1], mean_got.at[1], -1, 0),
+    ]
+    launch(mean_copies)
+
     def order(n):
         return ((((n & 127) + 32) & 127) << 2) + (n >> 7)
 
@@ -252,13 +331,7 @@
     lax.fori_loop(0, WIDE // 32, fill, 0)
     for ref in list(grid_p) + list(grid_q) + list(grid_b) + list(grid_wn) + [deep]:
         ref[...] = jnp.zeros_like(ref)
-    row_number = lax.broadcasted_iota(jnp.int32, (ROWS, LANES), 0)
-    place = (lat * ROWS + row_number).astype(jnp.float32)
-    angle = jnp.pi * ((place + 0.5) / (ROWS * lat_count) - 0.5)
-    turning = CORIOLIS * jnp.sin(angle)
-    rotation = jnp.concatenate([turning, turning], axis=1)
-
-    for copy in first:
+    for copy in column_copies:
         copy.wait_recv()
 
     west_tile, east_tile = cols_got.at[0], cols_got.at[1]
@@ -268,25 +341,45 @@
     launch(more_depth)
     depth_copies = depth_copies + more_depth
 
-    row = lax.broadcasted_iota(jnp.int32, (ROWS, COLS), 0)
-    column = lax.broadcasted_iota(jnp.int32, (ROWS, COLS), 1)
-    on_east, on_west = column == COLS - 1, column == 0
-    on_north, on_south = row == ROWS - 1, row == 0
-
-    def beside(values, east_edge, west_edge, north_edge, south_edge):
-        return (
-            jnp.where(on_east, east_edge, pltpu.roll(values, COLS - 1, 1)),
-            jnp.where(on_west, west_edge, pltpu.roll(values, 1, 1)),
-            jnp.where(on_north, north_edge, pltpu.roll(values, ROWS - 1, 0)),
-            jnp.where(on_south, south_edge, pltpu.roll(values, 1, 0)),
-        )
+    lane_row = lane8 & 3
+    lane_level = ((lane8 >> 2) & 7).astype(jnp.float32)
+
+    def packed(values, column):
+        result = zero8
+        for g in range(4):
+            result = jnp.where(lane_row == g, values[8 * g : 8 * g + 8, column : column + 1], result)
+        return result
+
+    def column_flux(own, other, own_depth, other_depth):
+        limit = jnp.minimum(own_depth, other_depth)
+        flux = jnp.where(lane_level < limit, other - own, 0.0)
+        for turn in (4, 8, 16):
+            flux = flux + pltpu.roll(flux, turn, 1)
+        flux = gain * flux
+        return [
+            jnp.concatenate([flux[:, at + g : at + g + 1] for g in range(4)], axis=0)
+            for at in (28, 60)
+        ]
+
+    east_flux = column_flux(
+        cols_send[0, 64:72, :],
+        east_tile[64:72, :],
+        packed(depth, COLS - 1),
+        packed(east_tile[0:32, :], 0),
+    )
+    west_flux = column_flux(
+        cols_send[1, 64:72, :],
+        west_tile[64:72, :],
+        packed(depth, 0),
+        packed(west_tile[0:32, :], LANES - 1),
+    )
 
     depth_near = beside(
         depth,
         east_tile[0:32, 0:1],
         west_tile[0:32, LANES - 1 : LANES],
-        rows_got[1, 24:25, :] * inside(1),
-        rows_got[0, 24:25, :] * inside(-1),
+        north_depth,
+        south_depth,
     )
     open_depth = [jnp.minimum(depth, near) for near in depth_near]
     east_edges = east_tile[64:72, :]
@@ -303,41 +396,7 @@
         south_edge = rows_got[0, pl.ds(8 * f + k, 1), :]
         return values, beside(values, east_edge, west_edge, north_edge, south_edge)
 
-    def laplace(faces, values, nearby):
-        terms = [jnp.where(face, near - values, 0.0) for face, near in zip(faces, nearby)]
-        return (terms[0] + terms[1]) + (terms[2] + terms[3])
-
-    def momentum(k, carry):
-        sum_u, sum_v = carry
-        level = k.astype(jnp.float32)
-        faces = [level < limit for limit in open_depth]
-        wet = level < depth
-        u, near_u = near_field(0, u_ref, k)
-        v, near_v = near_field(1, v_ref, k)
-        guess_u = u + TIME_STEP * (VISCOSITY * laplace(faces, u, near_u) + rotation * v)
-        guess_v = v + TIME_STEP * (VISCOSITY * laplace(faces, v, near_v) - rotation * u)
-        guess_u = jnp.where(wet, guess_u, 0.0)
-        guess_v = jnp.where(wet, guess_v, 0.0)
-        rows = pl.ds(pl.multiple_of(k * ROWS, ROWS), ROWS)
-        u_star[rows, :] = guess_u
-        v_star[rows, :] = guess_v
-        return sum_u + guess_u, sum_v + guess_v
-
-    zero = jnp.zeros((ROWS, COLS), jnp.float32)
-    sum_u, sum_v = lax.fori_loop(0, LEVELS, momentum, (zero, zero))
-    mean_u = sum_u * (1.0 / LEVELS)
-    mean_v = sum_v * (1.0 / LEVELS)
-    for side, tile in ((0, 1), (1, 0)):
-        cut = slice(tile * LANES, (tile + 1) * LANES)
-        mean_send[side, 0:32, :] = mean_u[:, cut]
-        mean_send[side, 32:64, :] = mean_v[:, cut]
-    mean_copies = [
-        send(mean_send.at[0], mean_got.at[0], 1, 0),
-        send(mean_send.at[1], mean_got.at[1], -1, 0),
-    ]
-    launch(mean_copies)
-
-    def tracer(k, carry):
+    def layer(k, carry):
         level = k.astype(jnp.float32)
         faces = [level < limit for limit in open_depth]
         t, near_t = near_field(2, t_ref, k)
@@ -352,25 +411,35 @@
             north * (t + near_t[2]) - south * (near_t[3] + t)
         )
         result = t + TIME_STEP * (DIFFUSIVITY * spread - 0.5 * transport)
+        guess_u, guess_v = momentum(faces, u, near_u, v, near_v)
+        wet = level < depth
         rows = pl.ds(pl.multiple_of(k * ROWS, ROWS), ROWS)
-        t_out[rows, :] = jnp.where(level < depth, result, 0.0)
+        u_star[rows, :] = jnp.where(wet, guess_u, 0.0)
+        v_star[rows, :] = jnp.where(wet, guess_v, 0.0)
+        t_out[rows, :] = jnp.where(wet, result, 0.0)
         return carry
 
-    lax.fori_loop(0, LEVELS, tracer, 0)
-    stores = [
-        pltpu.make_async_copy(near, far, load_sem.at[i])
-        for i, (near, far) in enumerate(
-            ((u_star, u_home), (v_star, v_home), (t_out, t_home))
-        )
-    ]
-    for store in stores:
-        store.start()
+    lax.fori_loop(0, EARLY_LEVELS, layer, 0)
 
     for copy in mean_copies:
         copy.wait_recv()
     west_mean, east_mean = mean_got.at[0], mean_got.at[1]
-    wide_u = jnp.concatenate([west_mean[0:32, :], mean_u, east_mean[0:32, :]], axis=1)
-    wide_v = jnp.concatenate([west_mean[32:64, :], mean_v, east_mean[32:64, :]], axis=1)
+    tile_lane = lax.broadcasted_iota(jnp.int32, (ROWS, LANES), 1)
+    tile_first, tile_last = tile_lane == 0, tile_lane == LANES - 1
+
+    def window(f, values):
+        cut = slice(32 * f, 32 * f + 32)
+        return jnp.concatenate(
+            [
+                west_mean[cut, :] - jnp.where(tile_last, west_flux[f], 0.0),
+                values[:, 0:LANES] + jnp.where(tile_first, west_flux[f], 0.0),
+                values[:, LANES:COLS] + jnp.where(tile_last, east_flux[f], 0.0),
+                east_mean[cut, :] - jnp.where(tile_first, east_flux[f], 0.0),
+            ],
+            axis=1,
+        )
+
+    wide_u, wide_v = window(0, mean_u), window(1, mean_v)
     wide_eta = jnp.concatenate([west_tile[32:64, :], elevation, east_tile[32:64, :]], axis=1)
     wide_row = lax.broadcasted_iota(jnp.int32, (ROWS, WIDE), 0)
     north_v = jnp.where(wide_row == ROWS - 1, 0.0, pltpu.roll(wide_v, ROWS - 1, 0))
@@ -499,6 +568,17 @@
         send(weight_send, weight_got.at[i], 0, move) for i, move in enumerate(LAT_MOVES)
     ]
     launch(weight_copies)
+
+    lax.fori_loop(EARLY_LEVELS, LEVELS, layer, 0)
+    stores = [
+        pltpu.make_async_copy(near, far, load_sem.at[i])
+        for i, (near, far) in enumerate(
+            ((u_star, u_home), (v_star, v_home), (t_out, t_home))
+        )
+    ]
+    for store in stores:
+        store.start()
+
 
     for copy in source_copies:
         copy.wait_recv()

time: 53.9 us -> 51.2 us (0.950)
  the two profiles are of different devices: /device:TPU:2 before, /device:TPU:32 now
where the time goes in v3:
time: 51.2 us; the launch traced here: 51 us
  Pallas kernels  50.4 us (98%)
  between operations  0.64 us (1%)
    pallas_call x1, Pallas kernels, shards(): pl.pallas_call(functools.partial(kernel, lon_count, lat_count), out_shape...  48.3 us
    pallas_call x1, Pallas kernels, shards(): pl.pallas_call(finish, out_shape=[jax.ShapeDtypeStruct(flat, f32)] * 3 +...  2.08 us

profile of v3, /device:TPU:32, one launch (start us, length us, event | category | flops | bytes accessed | tf_op | source)
XLA Modules:
  0.0 51.0 jit_solution(4613489563422480595)
XLA Ops:
  0.6 48.3 %shard_map.84 = (f32[256,256]{1,0:T(8,128)}, f32[256,256]{1,0:T(8,128)}, f32[256,256]{1,0:T(8,128)}, f32[32,256]{1,0:T(8,128)}, f32[32,256]{1,0:T(8,128)}, /*index=5*/f32[32,256]{1,0:T(8,128)}) custom-call(f32[256,256]{1,0:T(8,128)} %bitcast.6, f32[256,256]{1,0:T(8,128)} %bitcast.7, f32[256,256]{1,0:T(8,128)} %bitcast.8, s32[32,256]{1,0:T(8,128)} %depth_ref.1, ...), custom_call_target="tpu_custom_call" | custom-call | tf_op jit(solution)/shard_map/pallas_call | solution.py:771
  49.0 2.1 %shard_map.85 = (f32[256,256]{1,0:T(8,128)}, f32[256,256]{1,0:T(8,128)}, f32[256,256]{1,0:T(8,128)}, f32[32,256]{1,0:T(8,128)}) custom-call(f32[256,256]{1,0:T(8,128)} %get-tuple-element.14.u_star, f32[256,256]{1,0:T(8,128)} %get-tuple-element.15.v_star, f32[256,256]{1,0:T(8,128)} %get-tuple-element.16.t, f32[32,256]{1,0:T(8,128)} %get-tuple-element.17.p, ...), custom_call_target="tpu_custom_call" | custom-call | tf_op jit(solution)/shard_map/pallas_call | solution.py:824

commit v4 on v3

--- a/solution.py
+++ b/solution.py
@@ -74,6 +74,29 @@
     return (product[:count] + product[count : 2 * count]) + product[2 * count :]
 
 
+class Link:
+    def __init__(self, copy, leaves, comes):
+        self.copy, self.leaves, self.comes = copy, leaves, comes
+
+    def start(self):
+        if self.leaves is None:
+            self.copy.start()
+        else:
+            pl.when(self.leaves)(self.copy.start)
+
+    def wait_send(self):
+        if self.leaves is None:
+            self.copy.wait_send()
+        else:
+            pl.when(self.leaves)(self.copy.wait_send)
+
+    def wait_recv(self):
+        if self.comes is None:
+            self.copy.wait_recv()
+        else:
+            pl.when(self.comes)(self.copy.wait_recv)
+
+
 def kernel(
     lon_count,
     lat_count,
@@ -82,12 +105,10 @@
     t_far,
     depth_far,
     elevation_far,
-    u_home,
-    v_home,
-    t_home,
+    u_out,
+    v_out,
+    t_out,
     p_out,
-    push_u_out,
-    push_v_out,
     u_ref,
     v_ref,
     t_ref,
@@ -95,7 +116,6 @@
     elevation_ref,
     u_star,
     v_star,
-    t_out,
     rows_send,
     rows_got,
     cols_send,
@@ -142,7 +162,7 @@
 
     def send(source, target, lon_move, lat_move):
         at = next(sems)
-        return pltpu.make_async_remote_copy(
+        copy = pltpu.make_async_remote_copy(
             src_ref=source,
             dst_ref=target,
             send_sem=send_sem.at[at],
@@ -150,10 +170,17 @@
             device_id=there(lon_move, lat_move),
             device_id_type=MESH_IDS,
         )
+        if lat_move == 0:
+            return Link(copy, None, None)
+        return Link(copy, inside(lat_move), inside(-lat_move))
 
     def inside(lat_move):
-        spot = lat + lat_move
-        return jnp.where((spot >= 0) & (spot < lat_count), 1.0, 0.0).astype(jnp.float32)
+        return (lat + lat_move >= 0) & (lat + lat_move < lat_count)
+
+    def kept(lat_move, values):
+        if lat_move == 0:
+            return values
+        return jnp.where(inside(lat_move), values, jnp.zeros_like(values))
 
     started = []
 
@@ -163,10 +190,20 @@
         started.extend(copies)
 
     barrier = pltpu.get_barrier_semaphore()
-    for lon_move, lat_move in [(1, 0), (-1, 0)] + [(0, m) for m in LAT_MOVES]:
+    for lon_move in (1, -1):
         pl.semaphore_signal(
-            barrier, inc=1, device_id=there(lon_move, lat_move), device_id_type=MESH_IDS
+            barrier, inc=1, device_id=there(lon_move, 0), device_id_type=MESH_IDS
         )
+    beside_count = jnp.int32(2)
+    for lat_move in LAT_MOVES:
+        beside_count = beside_count + inside(lat_move).astype(jnp.int32)
+
+        @pl.when(inside(lat_move))
+        def _(lat_move=lat_move):
+            pl.semaphore_signal(
+                barrier, inc=1, device_id=there(0, lat_move), device_id_type=MESH_IDS
+            )
+
 
     loads = [
         pltpu.make_async_copy(far, near, load_sem.at[i])
@@ -215,7 +252,7 @@
         cols_send[side, 32:64, :] = elevation[:, cut]
         cols_send[side, 64:72, :] = edge
 
-    pl.semaphore_wait(barrier, 2 + len(LAT_MOVES))
+    pl.semaphore_wait(barrier, beside_count)
     row_copies = [
         send(rows_send.at[0], rows_got.at[0], 0, 1),
         send(rows_send.at[1], rows_got.at[1], 0, -1),
@@ -285,8 +322,8 @@
 
     for copy in row_copies:
         copy.wait_recv()
-    north_depth = rows_got[1, 24:25, :] * inside(1)
-    south_depth = rows_got[0, 24:25, :] * inside(-1)
+    north_depth = kept(1, rows_got[1, 24:25, :])
+    south_depth = kept(-1, rows_got[0, 24:25, :])
     level8 = lax.broadcasted_iota(jnp.int32, (LEVELS, COLS), 0).astype(jnp.float32)
 
     def row_flux(f, side, limit):
@@ -392,8 +429,8 @@
         west_lanes = pltpu.roll(west_edges, turn, 1)
         east_edge = jnp.concatenate([east_lanes[:, g : g + 1] for g in range(4)], axis=0)
         west_edge = jnp.concatenate([west_lanes[:, g : g + 1] for g in range(4)], axis=0)
-        north_edge = rows_got[1, pl.ds(8 * f + k, 1), :]
-        south_edge = rows_got[0, pl.ds(8 * f + k, 1), :]
+        north_edge = kept(1, rows_got[1, pl.ds(8 * f + k, 1), :])
+        south_edge = kept(-1, rows_got[0, pl.ds(8 * f + k, 1), :])
         return values, beside(values, east_edge, west_edge, north_edge, south_edge)
 
     def layer(k, carry):
@@ -461,12 +498,16 @@
     source_copies = [
         send(ends_send, ends_got.at[i], 0, move) for i, move in enumerate(LAT_MOVES)
     ] + [
-        send(source_send, source_got.at[0], 0, 1),
-        send(source_send, source_got.at[1], 0, -1),
+        send(source_send.at[:, pl.ds(24, 8)], source_got.at[0, :, pl.ds(24, 8)], 0, 1),
+        send(source_send.at[:, pl.ds(0, 8)], source_got.at[1, :, pl.ds(0, 8)], 0, -1),
+    ]
+    far_copies = [
+        send(source_send.at[:, pl.ds(0, 24)], source_got.at[0, :, pl.ds(0, 24)], 0, 1),
+        send(source_send.at[:, pl.ds(8, 24)], source_got.at[1, :, pl.ds(8, 24)], 0, -1),
         send(source_send.at[:, pl.ds(ROWS - 8, 8)], source_got_far.at[0], 0, 2),
         send(source_send.at[:, pl.ds(0, 8)], source_got_far.at[1], 0, -2),
     ]
-    launch(source_copies)
+    launch(source_copies + far_copies)
 
     for copy in depth_copies:
         copy.wait_recv()
@@ -474,15 +515,15 @@
     def slot_of(lat_move):
         return LAT_MOVES.index(-lat_move)
 
-    def wide_depth(own, halo, mask):
-        return mask * jnp.concatenate([halo[:, 0:LANES], own, halo[:, LANES:COLS]], axis=1)
+    def wide_depth(own, halo, move):
+        return kept(move, jnp.concatenate([halo[:, 0:LANES], own, halo[:, LANES:COLS]], axis=1))
 
     blocks = [
-        wide_depth(deep_got_far[0, 0], deep_got_far[1, 0], inside(-2)),
-        wide_depth(deep_got[0, 0], deep_got[1, 0], inside(-1)),
-        wide_depth(deep_send[0], deep_send[1], 1.0),
-        wide_depth(deep_got[0, 1], deep_got[1, 1], inside(1)),
-        wide_depth(deep_got_far[0, 1], deep_got_far[1, 1], inside(2)),
+        wide_depth(deep_got_far[0, 0], deep_got_far[1, 0], -2),
+        wide_depth(deep_got[0, 0], deep_got[1, 0], -1),
+        wide_depth(deep_send[0], deep_send[1], 0),
+        wide_depth(deep_got[0, 1], deep_got[1, 1], 1),
+        wide_depth(deep_got_far[0, 1], deep_got_far[1, 1], 2),
     ]
     by_class = jnp.dot(
         jnp.concatenate(blocks, axis=0).astype(jnp.bfloat16),
@@ -553,7 +594,7 @@
 
     def around(held, own, got, moves):
         def block(move):
-            return got[moves.index(-move)][...] * inside(move)
+            return kept(move, got[moves.index(-move)][...])
 
         held[0, pl.ds(ORIGIN[3], 8), :] = jnp.where(upper, pltpu.roll(block(1), 4, 0), own)
         lower = pltpu.roll(block(-1), 4, 0)
@@ -570,16 +611,6 @@
     launch(weight_copies)
 
     lax.fori_loop(EARLY_LEVELS, LEVELS, layer, 0)
-    stores = [
-        pltpu.make_async_copy(near, far, load_sem.at[i])
-        for i, (near, far) in enumerate(
-            ((u_star, u_home), (v_star, v_home), (t_out, t_home))
-        )
-    ]
-    for store in stores:
-        store.start()
-
-
     for copy in source_copies:
         copy.wait_recv()
 
@@ -587,23 +618,30 @@
 
     def ends(move, spot):
         held = ends_send if move == 0 else ends_got.at[slot_of(move)]
-        return held[spot : spot + 1, :] * (0.5 * inside(move))
-
-    def place_source(c, move, first, values):
-        rows = pl.ds(ORIGIN[0] + first, values.shape[0])
-        at = rows32[: values.shape[0]] + (first - 32 * move)
-        if move < 2:
-            values = values - jnp.where(at == ROWS - 1, ends(move + 1, c), 0.0)
-        if move > -2:
-            values = values + jnp.where(at == 0, ends(move - 1, 4 + c), 0.0)
-        grid_b[0][c, rows, :] = jnp.where(deep[c, rows, :] > 0.5, values, 0.0)
-
-    for c in range(4):
-        place_source(c, -2, -40, source_got_far[0, c])
-        place_source(c, -1, -32, source_got[0, c])
-        place_source(c, 0, 0, source_send[c])
-        place_source(c, 1, 32, source_got[1, c])
-        place_source(c, 2, 64, source_got_far[1, c])
+        return 0.5 * kept(move, held[spot : spot + 1, :])
+
+    def place_source(move, low, high, held):
+        at = rows32[: high - low] + low
+        for c in range(4):
+            rows = pl.ds(ORIGIN[0] + 32 * move + low, high - low)
+            values = held[c]
+            if move < 2 and high == ROWS:
+                values = values - jnp.where(at == ROWS - 1, ends(move + 1, c), 0.0)
+            if move > -2 and low == 0:
+                values = values + jnp.where(at == 0, ends(move - 1, 4 + c), 0.0)
+            grid_b[0][c, rows, :] = jnp.where(deep[c, rows, :] > 0.5, values, 0.0)
+
+    place_source(-1, 24, 32, source_got.at[0, :, pl.ds(24, 8)])
+    place_source(0, 0, 32, source_send)
+    place_source(1, 0, 8, source_got.at[1, :, pl.ds(0, 8)])
+
+    def place_far_source():
+        for copy in far_copies:
+            copy.wait_recv()
+        place_source(-2, 24, 32, source_got_far.at[0])
+        place_source(-1, 0, 24, source_got.at[0, :, pl.ds(0, 24)])
+        place_source(1, 8, 32, source_got.at[1, :, pl.ds(8, 24)])
+        place_source(2, 0, 8, source_got_far.at[1])
 
     def operator(g, held, at):
         rows, after, before = pl.ds(at, 8), pl.ds(at + 1, 8), pl.ds(at - 1, 8)
@@ -679,24 +717,29 @@
 
         each_chunk(*span(g + 1, first, last), body)
 
-    def coarse_source(cycle, reach):
+    def coarse_links(cycle, reach):
         coarse_send[cycle] = grid_b[3][0, pl.ds(ORIGIN[3], 8), :]
         moves = LAT_MOVES[: 2 * reach]
-        got = coarse_got.at[pl.ds(4 * cycle, 2 * reach)]
         copies = [
-            send(coarse_send.at[cycle], got.at[i], 0, move) for i, move in enumerate(moves)
+            send(coarse_send.at[cycle], coarse_got.at[4 * cycle + i], 0, move)
+            for i, move in enumerate(moves)
         ]
         launch(copies)
-        if cycle == 0:
-            for copy in weight_copies:
-                copy.wait_recv()
-            for held, first in ((grid_we[3], 0), (grid_wn[3], 8)):
-                cut = pl.ds(first, 8)
-                around(held, weight_send[cut, :], [weight_got.at[i, cut] for i in range(4)], LAT_MOVES)
-            each_chunk(ORIGIN[3] - 8, ORIGIN[3] + 16, lambda at: finish_weights(3, pl.ds(at, 8)))
+        return copies, moves
+
+    def coarse_weights_around():
+        for copy in weight_copies:
+            copy.wait_recv()
+        for held, first in ((grid_we[3], 0), (grid_wn[3], 8)):
+            cut = pl.ds(first, 8)
+            around(held, weight_send[cut, :], [weight_got.at[i, cut] for i in range(4)], LAT_MOVES)
+        each_chunk(ORIGIN[3] - 8, ORIGIN[3] + 16, lambda at: finish_weights(3, pl.ds(at, 8)))
+
+    def coarse_source(cycle, copies, moves):
         for copy in copies:
             copy.wait_recv()
-        around(grid_b[3], coarse_send[cycle], [got.at[i] for i in range(2 * reach)], moves)
+        got = [coarse_got.at[4 * cycle + i] for i in range(len(moves))]
+        around(grid_b[3], coarse_send[cycle], got, moves)
 
     plans = (
         ((-40, 72), (-24, 40), (-16, 24), (-8, 16), (-16, 32), (-24, 56)),
@@ -705,16 +748,28 @@
     )
     for cycle in range(CYCLES):
         before0, down1, down2, up2, up1, after0 = plans[cycle]
+
+        def first_leg(before0, down1, down2, cycle=cycle):
+            if cycle == 0:
+                from_zero(0, *before0, grid_q[0])
+            else:
+                sweep(0, *before0, grid_p[0], grid_q[0])
+            restricted(0, *before0, grid_q[0])
+            from_zero(1, *down1, grid_q[1])
+            restricted(1, *down1, grid_q[1])
+            from_zero(2, *down2, grid_q[2])
+
         if cycle == 0:
-            from_zero(0, *before0, grid_q[0])
+            first_leg((-8, 40), (-8, 24), (-8, 16))
         else:
-            sweep(0, *before0, grid_p[0], grid_q[0])
-        restricted(0, *before0, grid_q[0])
-        from_zero(1, *down1, grid_q[1])
-        restricted(1, *down1, grid_q[1])
-        from_zero(2, *down2, grid_q[2])
+            first_leg(before0, down1, down2)
         restricted(2, -8, 16, grid_q[2])
-        coarse_source(cycle, 1 if cycle == 2 else 2)
+        links = coarse_links(cycle, 1 if cycle == 2 else 2)
+        if cycle == 0:
+            place_far_source()
+            first_leg(before0, down1, down2)
+            coarse_weights_around()
+        coarse_source(cycle, *links)
         from_zero(3, -8, 16, grid_q[3])
         here, there_ = grid_q[3], grid_p[3]
         for _ in range(SWEEPS - 1):
@@ -740,23 +795,24 @@
     )
     ordered = exact_select(stacked, unchoice[...])
     p_out[...] = ordered[0:32]
-    push_u_out[...] = GRAVITY_STEP * ordered[32:64]
-    push_v_out[...] = GRAVITY_STEP * ordered[64:96]
-    for store in stores:
-        store.wait()
-    for copy in started:
-        copy.wait_send()
-
-
-def finish(u_star, v_star, t, p, push_u, push_v, depth_ref, u_out, v_out, t_out, p_out):
-    depth = depth_ref[...]
-    p_out[...] = p[...]
-    t_out[...] = t[...]
+    push_u = GRAVITY_STEP * ordered[32:64]
+    push_v = GRAVITY_STEP * ordered[64:96]
     for k in range(LEVELS):
         rows = slice(k * ROWS, (k + 1) * ROWS)
         wet = depth > k
-        u_out[rows, :] = jnp.where(wet, u_star[rows, :] - push_u[...], 0.0)
-        v_out[rows, :] = jnp.where(wet, v_star[rows, :] - push_v[...], 0.0)
+        u_out[rows, :] = jnp.where(wet, u_star[rows, :] - push_u, 0.0)
+        v_out[rows, :] = jnp.where(wet, v_star[rows, :] - push_v, 0.0)
+    for copy in started:
+        copy.wait_send()
+
+
+def deliver(*refs):
+    held, outs, sem = refs[:4], refs[4:8], refs[8]
+    copies = [pltpu.make_async_copy(held[i], outs[i], sem.at[i]) for i in range(4)]
+    for copy in copies:
+        copy.start()
+    for copy in copies:
+        copy.wait()
 
 
 def shards(lon_count, lat_count, u, v, t, depth, elevation):
@@ -767,20 +823,19 @@
     def grids(classes=CLASSES):
         return [pltpu.VMEM((c, h, LANES), f32) for c, h in zip(classes, HEIGHT)]
 
+    shapes = [flat] * 3 + [(ROWS, COLS)]
     anywhere = pl.BlockSpec(memory_space=pl.ANY)
     held = pl.pallas_call(
         functools.partial(kernel, lon_count, lat_count),
-        out_shape=[jax.ShapeDtypeStruct(flat, f32)] * 3
-        + [jax.ShapeDtypeStruct((ROWS, COLS), f32)] * 3,
+        out_shape=[pltpu.VMEM(shape, f32) for shape in shapes],
         in_specs=[anywhere] * 5,
-        out_specs=[anywhere] * 3 + [block] * 3,
+        out_specs=[block] * 4,
         scratch_shapes=[
             pltpu.VMEM(flat, f32),
             pltpu.VMEM(flat, f32),
             pltpu.VMEM(flat, f32),
             pltpu.VMEM((ROWS, COLS), jnp.int32),
             pltpu.VMEM((ROWS, COLS), f32),
-            pltpu.VMEM(flat, f32),
             pltpu.VMEM(flat, f32),
             pltpu.VMEM(flat, f32),
             pltpu.VMEM((2, 32, COLS), f32),
@@ -818,17 +873,21 @@
             pltpu.SemaphoreType.DMA((40,)),
         ],
         compiler_params=pltpu.CompilerParams(
-            collective_id=0, has_side_effects=True, vmem_limit_bytes=60 << 20
+            collective_id=0, has_side_effects=True, vmem_limit_bytes=32 << 20
         ),
-    )(u.reshape(flat), v.reshape(flat), t.reshape(flat), depth, elevation)
+    )(
+        *[
+            pltpu.with_memory_space_constraint(x, pltpu.HBM)
+            for x in (u.reshape(flat), v.reshape(flat), t.reshape(flat), depth, elevation)
+        ]
+    )
     outs = pl.pallas_call(
-        finish,
-        out_shape=[jax.ShapeDtypeStruct(flat, f32)] * 3
-        + [jax.ShapeDtypeStruct((ROWS, COLS), f32)],
-        in_specs=[block] * 7,
-        out_specs=[block] * 4,
-        compiler_params=pltpu.CompilerParams(vmem_limit_bytes=60 << 20),
-    )(*held, depth)
+        deliver,
+        out_shape=[jax.ShapeDtypeStruct(shape, f32) for shape in shapes],
+        in_specs=[block] * 4,
+        out_specs=[anywhere] * 4,
+        scratch_shapes=[pltpu.SemaphoreType.DMA((4,))],
+    )(*[pltpu.with_memory_space_constraint(x, pltpu.VMEM) for x in held])
     shape = (LEVELS, ROWS, COLS)
     return outs[0].reshape(shape), outs[1].reshape(shape), outs[2].reshape(shape), outs[3]
 

time: 51.2 us -> 45.2 us (0.88)
  the two profiles are of different devices: /device:TPU:32 before, /device:TPU:4 now
where the time goes in v4:
time: 45.2 us; the launch traced here: 45.1 us
  Pallas kernels  44.4 us (98%)
  between operations  0.64 us (1%)
    pallas_call x1, Pallas kernels, shards(): pl.pallas_call(functools.partial(kernel, lon_count, lat_count), out_shape...  43.5 us
    pallas_call x1, Pallas kernels, shards(): pl.pallas_call(deliver, out_shape=[jax.ShapeDtypeStruct(shape, f32) for s...  0.91 us

profile of v4, /device:TPU:4, one launch (start us, length us, event | category | flops | bytes accessed | tf_op | source)
XLA Modules:
  0.0 45.1 jit_solution(5463811505316517824)
XLA Ops:
  0.6 43.5 %shard_map.84 = (f32[256,256]{1,0:T(8,128)S(1)}, f32[256,256]{1,0:T(8,128)S(1)}, f32[256,256]{1,0:T(8,128)S(1)}, f32[32,256]{1,0:T(8,128)S(1)}) custom-call(f32[256,256]{1,0:T(8,128)} %bitcast.6, f32[256,256]{1,0:T(8,128)} %bitcast.7, f32[256,256]{1,0:T(8,128)} %bitcast.8, s32[32,256]{1,0:T(8,128)} %depth_far.1, f32[32,256]{1,0:T(8,128)} %elevation_far.1), custom_call_target="tpu_custom_call" | custom-call | tf_op jit(solution)/shard_map/pallas_call | solution.py:828
  44.2 0.9 %shard_map.85 = (f32[256,256]{1,0:T(8,128)}, f32[256,256]{1,0:T(8,128)}, f32[256,256]{1,0:T(8,128)}, f32[32,256]{1,0:T(8,128)}) custom-call(f32[256,256]{1,0:T(8,128)S(1)} %get-tuple-element.12.refs_0_, f32[256,256]{1,0:T(8,128)S(1)} %get-tuple-element.13.refs_1_, f32[256,256]{1,0:T(8,128)S(1)} %get-tuple-element.14.refs_2_, ...), custom_call_target="tpu_custom_call" | custom-call | tf_op jit(solution)/shard_map/pallas_call | solution.py:884

commit v5 on v4

--- a/solution.py
+++ b/solution.py
@@ -30,7 +30,7 @@
 MASS = tuple(MASS_TERM * 4.0**g for g in range(4))
 
 LAT_MOVES = (1, -1, 2, -2)
-EARLY_LEVELS = 3
+EARLY_LEVELS = 5
 
 
 def east_of(parts, step):
@@ -128,8 +128,8 @@
     source_send,
     source_got,
     source_got_far,
-    ends_send,
-    ends_got,
+    close_send,
+    close_got,
     weight_send,
     weight_got,
     coarse_send,
@@ -146,6 +146,7 @@
     grid_dg,
     grid_iv,
     grid_r,
+    grid_s,
     load_sem,
     send_sem,
     recv_sem,
@@ -366,7 +367,7 @@
         return carry
 
     lax.fori_loop(0, WIDE // 32, fill, 0)
-    for ref in list(grid_p) + list(grid_q) + list(grid_b) + list(grid_wn) + [deep]:
+    for ref in list(grid_p) + list(grid_q) + list(grid_b) + list(grid_wn) + [deep, grid_s]:
         ref[...] = jnp.zeros_like(ref)
     for copy in column_copies:
         copy.wait_recv()
@@ -493,15 +494,18 @@
     for c in range(4):
         cut = slice(LANES * c, LANES * (c + 1))
         source_send[c] = by_class[0:32, cut]
-        ends_send[c : c + 1, :] = by_class[32:33, cut]
-        ends_send[4 + c : 5 + c, :] = by_class[33:34, cut]
+        close_send[0, c] = by_class[24:32, cut]
+        close_send[1, c] = by_class[0:8, cut]
+        for side in (0, 1):
+            close_send[side, 4, c : c + 1, :] = by_class[32:33, cut]
+            close_send[side, 4, 4 + c : 5 + c, :] = by_class[33:34, cut]
     source_copies = [
-        send(ends_send, ends_got.at[i], 0, move) for i, move in enumerate(LAT_MOVES)
-    ] + [
-        send(source_send.at[:, pl.ds(24, 8)], source_got.at[0, :, pl.ds(24, 8)], 0, 1),
-        send(source_send.at[:, pl.ds(0, 8)], source_got.at[1, :, pl.ds(0, 8)], 0, -1),
+        send(close_send.at[0], close_got.at[0], 0, 1),
+        send(close_send.at[1], close_got.at[1], 0, -1),
     ]
     far_copies = [
+        send(close_send.at[0, 4], close_got.at[2, 4], 0, 2),
+        send(close_send.at[1, 4], close_got.at[3, 4], 0, -2),
         send(source_send.at[:, pl.ds(0, 24)], source_got.at[0, :, pl.ds(0, 24)], 0, 1),
         send(source_send.at[:, pl.ds(8, 24)], source_got.at[1, :, pl.ds(8, 24)], 0, -1),
         send(source_send.at[:, pl.ds(ROWS - 8, 8)], source_got_far.at[0], 0, 2),
@@ -617,7 +621,7 @@
     rows32 = lax.broadcasted_iota(jnp.int32, (ROWS, LANES), 0)
 
     def ends(move, spot):
-        held = ends_send if move == 0 else ends_got.at[slot_of(move)]
+        held = close_send.at[0, 4] if move == 0 else close_got.at[slot_of(move), 4]
         return 0.5 * kept(move, held[spot : spot + 1, :])
 
     def place_source(move, low, high, held):
@@ -631,9 +635,9 @@
                 values = values + jnp.where(at == 0, ends(move - 1, 4 + c), 0.0)
             grid_b[0][c, rows, :] = jnp.where(deep[c, rows, :] > 0.5, values, 0.0)
 
-    place_source(-1, 24, 32, source_got.at[0, :, pl.ds(24, 8)])
+    place_source(-1, 24, 32, close_got.at[0])
     place_source(0, 0, 32, source_send)
-    place_source(1, 0, 8, source_got.at[1, :, pl.ds(0, 8)])
+    place_source(1, 0, 8, close_got.at[1])
 
     def place_far_source():
         for copy in far_copies:
@@ -741,48 +745,70 @@
         got = [coarse_got.at[4 * cycle + i] for i in range(len(moves))]
         around(grid_b[3], coarse_send[cycle], got, moves)
 
-    plans = (
-        ((-40, 72), (-24, 40), (-16, 24), (-8, 16), (-16, 32), (-24, 56)),
-        ((-24, 56), (-16, 32), (-8, 16), (-8, 16), (-8, 24), (-16, 48)),
-        ((-16, 48), (-8, 24), (-8, 16), (-8, 16), (-8, 24), (-8, 40)),
+    reach_before = (
+        ((-40, 72), (-24, 40), (-16, 24)),
+        ((-24, 56), (-16, 32), (-8, 16)),
+        ((-16, 48), (-8, 24), (-8, 16)),
     )
+    reach_after = ((-24, 56), (-16, 48), (-8, 40))
+    up_rows = ((-16, 32), (-8, 24), (-8, 24))
+    smoothed = (grid_q[0], grid_s, grid_q[0])
+    pressure = grid_p[0]
+
+    def descend(cycle, ranges):
+        for low, high in ranges[0]:
+            restricted(0, low, high, smoothed[cycle])
+        for low, high in ranges[1]:
+            from_zero(1, low, high, grid_q[1])
+        for low, high in ranges[1]:
+            restricted(1, low, high, grid_q[1])
+        for low, high in ranges[2]:
+            from_zero(2, low, high, grid_q[2])
+
+    def send_coarse(cycle):
+        descend(cycle, (((-8, 40),), ((-8, 24),), ((-8, 16),)))
+        restricted(2, -8, 16, grid_q[2])
+        return coarse_links(cycle, 1 if cycle == 2 else 2)
+
+    def outer(cycle):
+        parts = [((low, 0), (32 >> g, high)) for g, (low, high) in enumerate(reach_before[cycle])]
+        if cycle == 0:
+            for low, high in parts[0]:
+                from_zero(0, low, high, smoothed[0])
+        else:
+            for low, high in parts[0]:
+                sweep(0, low, high, pressure, smoothed[cycle])
+        descend(cycle, parts)
+
+    from_zero(0, -8, 40, smoothed[0])
+    links = send_coarse(0)
+    place_far_source()
+    outer(0)
+    coarse_weights_around()
     for cycle in range(CYCLES):
-        before0, down1, down2, up2, up1, after0 = plans[cycle]
-
-        def first_leg(before0, down1, down2, cycle=cycle):
-            if cycle == 0:
-                from_zero(0, *before0, grid_q[0])
-            else:
-                sweep(0, *before0, grid_p[0], grid_q[0])
-            restricted(0, *before0, grid_q[0])
-            from_zero(1, *down1, grid_q[1])
-            restricted(1, *down1, grid_q[1])
-            from_zero(2, *down2, grid_q[2])
-
-        if cycle == 0:
-            first_leg((-8, 40), (-8, 24), (-8, 16))
-        else:
-            first_leg(before0, down1, down2)
-        restricted(2, -8, 16, grid_q[2])
-        links = coarse_links(cycle, 1 if cycle == 2 else 2)
-        if cycle == 0:
-            place_far_source()
-            first_leg(before0, down1, down2)
-            coarse_weights_around()
         coarse_source(cycle, *links)
         from_zero(3, -8, 16, grid_q[3])
         here, there_ = grid_q[3], grid_p[3]
         for _ in range(SWEEPS - 1):
             sweep(3, -8, 16, here, there_)
             here, there_ = there_, here
-        corrected(2, *up2, grid_q[2], here)
-        sweep(2, *up2, grid_q[2], grid_p[2])
-        corrected(1, *up1, grid_q[1], grid_p[2])
-        sweep(1, *up1, grid_q[1], grid_p[1])
-        corrected(0, *after0, grid_q[0], grid_p[1])
-        sweep(0, *after0, grid_q[0], grid_p[0])
-
-    pressure = grid_p[0]
+        corrected(2, -8, 16, grid_q[2], here)
+        sweep(2, -8, 16, grid_q[2], grid_p[2])
+        corrected(1, *up_rows[cycle], grid_q[1], grid_p[2])
+        sweep(1, *up_rows[cycle], grid_q[1], grid_p[1])
+        corrected(0, -16, 48, smoothed[cycle], grid_p[1])
+        sweep(0, -8, 40, smoothed[cycle], pressure)
+        if cycle + 1 < CYCLES:
+            sweep(0, -8, 40, pressure, smoothed[cycle + 1])
+            links = send_coarse(cycle + 1)
+            low, high = reach_after[cycle]
+            if cycle == 0:
+                corrected(0, -32, -16, smoothed[0], grid_p[1])
+                corrected(0, 48, 64, smoothed[0], grid_p[1])
+            sweep(0, low, -8, smoothed[cycle], pressure)
+            sweep(0, 40, high, smoothed[cycle], pressure)
+            outer(cycle + 1)
+
     own = pl.ds(ORIGIN[0], ROWS)
     p = [pressure[c, own, :] for c in range(4)]
     slope_east = [0.5 * (e - w) for e, w in zip(east_of(p, 1), west_of(p, 1))]
@@ -850,8 +876,8 @@
             pltpu.VMEM((4, ROWS, LANES), f32),
             pltpu.VMEM((2, 4, ROWS, LANES), f32),
             pltpu.VMEM((2, 4, 8, LANES), f32),
-            pltpu.VMEM((8, LANES), f32),
-            pltpu.VMEM((4, 8, LANES), f32),
+            pltpu.VMEM((2, 5, 8, LANES), f32),
+            pltpu.VMEM((4, 5, 8, LANES), f32),
             pltpu.VMEM((16, LANES), f32),
             pltpu.VMEM((4, 16, LANES), f32),
             pltpu.VMEM((CYCLES, 8, LANES), f32),
@@ -868,6 +894,7 @@
             grids(),
             grids(),
             grids(),
+            pltpu.VMEM((4, HEIGHT[0], LANES), f32),
             pltpu.SemaphoreType.DMA((5,)),
             pltpu.SemaphoreType.DMA((40,)),
             pltpu.SemaphoreType.DMA((40,)),

time: 45.2 us -> 44.6 us (0.987)
  the two profiles are of different devices: /device:TPU:4 before, /device:TPU:2 now
where the time goes in v5:
time: 44.6 us; the launch traced here: 44.5 us
  Pallas kernels  43.9 us (98%)
  between operations  0.64 us (1%)
    pallas_call x1, Pallas kernels, shards(): pl.pallas_call(functools.partial(kernel, lon_count, lat_count), out_shape...  42.9 us
    pallas_call x1, Pallas kernels, shards(): pl.pallas_call(deliver, out_shape=[jax.ShapeDtypeStruct(shape, f32) for s...  0.91 us

profile of v5, /device:TPU:2, one launch (start us, length us, event | category | flops | bytes accessed | tf_op | source)
XLA Modules:
  0.0 44.5 jit_solution(5919843657285355355)
XLA Ops:
  0.6 42.9 %shard_map.84 = (f32[256,256]{1,0:T(8,128)S(1)}, f32[256,256]{1,0:T(8,128)S(1)}, f32[256,256]{1,0:T(8,128)S(1)}, f32[32,256]{1,0:T(8,128)S(1)}) custom-call(f32[256,256]{1,0:T(8,128)} %bitcast.6, f32[256,256]{1,0:T(8,128)} %bitcast.7, f32[256,256]{1,0:T(8,128)} %bitcast.8, s32[32,256]{1,0:T(8,128)} %depth_far.1, f32[32,256]{1,0:T(8,128)} %elevation_far.1), custom_call_target="tpu_custom_call" | custom-call | tf_op jit(solution)/shard_map/pallas_call | solution.py:854
  43.6 0.9 %shard_map.85 = (f32[256,256]{1,0:T(8,128)}, f32[256,256]{1,0:T(8,128)}, f32[256,256]{1,0:T(8,128)}, f32[32,256]{1,0:T(8,128)}) custom-call(f32[256,256]{1,0:T(8,128)S(1)} %get-tuple-element.12.refs_0_, f32[256,256]{1,0:T(8,128)S(1)} %get-tuple-element.13.refs_1_, f32[256,256]{1,0:T(8,128)S(1)} %get-tuple-element.14.refs_2_, ...), custom_call_target="tpu_custom_call" | custom-call | tf_op jit(solution)/shard_map/pallas_call | solution.py:911

commit v6 on v5

--- a/solution.py
+++ b/solution.py
@@ -26,7 +26,7 @@
 CLASSES = (4, 2, 1, 1)
 STEP = (1, 1, 1, 2)
 ORIGIN = (48, 32, 24, 16)
-HEIGHT = (128, 80, 56, 40)
+HEIGHT = (144, 96, 64, 48)
 MASS = tuple(MASS_TERM * 4.0**g for g in range(4))
 
 LAT_MOVES = (1, -1, 2, -2)

time: 44.6 us -> 44.7 us (level)
  no operation moved by 1% of the time
where the time goes in v6:
time: 44.7 us; the launch traced here: 44.5 us
  Pallas kernels  43.9 us (98%)
  between operations  0.64 us (1%)
    pallas_call x1, Pallas kernels, shards(): pl.pallas_call(functools.partial(kernel, lon_count, lat_count), out_shape...  43 us
    pallas_call x1, Pallas kernels, shards(): pl.pallas_call(deliver, out_shape=[jax.ShapeDtypeStruct(shape, f32) for s...  0.91 us

profile of v6, /device:TPU:2, one launch (start us, length us, event | category | flops | bytes accessed | tf_op | source)
XLA Modules:
  0.0 44.5 jit_solution(14602606018190639056)
XLA Ops:
  0.6 43.0 %shard_map.84 = (f32[256,256]{1,0:T(8,128)S(1)}, f32[256,256]{1,0:T(8,128)S(1)}, f32[256,256]{1,0:T(8,128)S(1)}, f32[32,256]{1,0:T(8,128)S(1)}) custom-call(f32[256,256]{1,0:T(8,128)} %bitcast.6, f32[256,256]{1,0:T(8,128)} %bitcast.7, f32[256,256]{1,0:T(8,128)} %bitcast.8, s32[32,256]{1,0:T(8,128)} %depth_far.1, f32[32,256]{1,0:T(8,128)} %elevation_far.1), custom_call_target="tpu_custom_call" | custom-call | tf_op jit(solution)/shard_map/pallas_call | solution.py:854
  43.6 0.9 %shard_map.85 = (f32[256,256]{1,0:T(8,128)}, f32[256,256]{1,0:T(8,128)}, f32[256,256]{1,0:T(8,128)}, f32[32,256]{1,0:T(8,128)}) custom-call(f32[256,256]{1,0:T(8,128)S(1)} %get-tuple-element.12.refs_0_, f32[256,256]{1,0:T(8,128)S(1)} %get-tuple-element.13.refs_1_, f32[256,256]{1,0:T(8,128)S(1)} %get-tuple-element.14.refs_2_, ...), custom_call_target="tpu_custom_call" | custom-call | tf_op jit(solution)/shard_map/pallas_call | solution.py:911

commit v7 on v6

--- a/solution.py
+++ b/solution.py
@@ -43,7 +43,7 @@
     return [turned] + list(parts[:-1])
 
 
-def each_chunk(first, last, body, unroll=5):
+def each_chunk(first, last, body, unroll=6):
     count = (last - first) // 8
     if count <= unroll:
         for i in range(count):

time: 44.7 us -> 43.9 us (0.982)
  the two profiles are of different devices: /device:TPU:2 before, /device:TPU:4 now
where the time goes in v7:
time: 43.9 us; the launch traced here: 43.8 us
  Pallas kernels  43.1 us (98%)
  between operations  0.64 us (1%)
    pallas_call x1, Pallas kernels, shards(): pl.pallas_call(functools.partial(kernel, lon_count, lat_count), out_shape...  42.2 us
    pallas_call x1, Pallas kernels, shards(): pl.pallas_call(deliver, out_shape=[jax.ShapeDtypeStruct(shape, f32) for s...  0.91 us

profile of v7, /device:TPU:4, one launch (start us, length us, event | category | flops | bytes accessed | tf_op | source)
XLA Modules:
  0.0 43.8 jit_solution(12736429602569637877)
XLA Ops:
  0.6 42.2 %shard_map.84 = (f32[256,256]{1,0:T(8,128)S(1)}, f32[256,256]{1,0:T(8,128)S(1)}, f32[256,256]{1,0:T(8,128)S(1)}, f32[32,256]{1,0:T(8,128)S(1)}) custom-call(f32[256,256]{1,0:T(8,128)} %bitcast.6, f32[256,256]{1,0:T(8,128)} %bitcast.7, f32[256,256]{1,0:T(8,128)} %bitcast.8, s32[32,256]{1,0:T(8,128)} %depth_far.1, f32[32,256]{1,0:T(8,128)} %elevation_far.1), custom_call_target="tpu_custom_call" | custom-call | tf_op jit(solution)/shard_map/pallas_call | solution.py:854
  42.9 0.9 %shard_map.85 = (f32[256,256]{1,0:T(8,128)}, f32[256,256]{1,0:T(8,128)}, f32[256,256]{1,0:T(8,128)}, f32[32,256]{1,0:T(8,128)}) custom-call(f32[256,256]{1,0:T(8,128)S(1)} %get-tuple-element.12.refs_0_, f32[256,256]{1,0:T(8,128)S(1)} %get-tuple-element.13.refs_1_, f32[256,256]{1,0:T(8,128)S(1)} %get-tuple-element.14.refs_2_, ...), custom_call_target="tpu_custom_call" | custom-call | tf_op jit(solution)/shard_map/pallas_call | solution.py:911
